TPU v7x, 512 devices: a whole 4x8x8 slice. The times are simulated.
512 devices in a mesh: leaf: 64 (over y, z), near: 8 (over x, core).
Axes of the slice: x: 4, y: 8, z: 8, core: 2. Of those that a mesh axis runs over, the one named last changes fastest.
Arguments:
- particles: float32 [4, 16, 64, 2048], P(None, None, 'leaf', 'near'), may hold values from -1 to 1
- counts: int32 [64, 2048], P('leaf', 'near'), may hold values from 1 to 16, as said below
- neighbours: int32 [64, 6, 2048], P('leaf', None, 'near'), may hold values from 0 to 271, as said below
- pattern: int32 [64, 7, 32, 256], P('leaf', None, None, 'near'), may hold values from 0 to 8
- kernels: bfloat16 [8, 512, 512], replicated, may hold values from -0.046875 to 0.046875
Outputs:
- potential: float32 [16, 64, 2048], P(None, 'leaf', 'near')
- local_exp: float32 [64, 256, 512], P('leaf', 'near')
Inputs may be any that keep to these rules, and one draw needn't show every extreme that they name: `counts`: each device's block of leaves holds at least one leaf with all 16 slots in use. `neighbours`: entry t of the list of a slab's leaf c equals c + 8 + d with d from -8 to 8. `pattern`: 0 marks no interaction; o + 1 marks kernels[o].
All inputs are finite; a program needn't handle non-finite values.
Results may differ from a plain program's by a relative error of at most 0.0003.
Values sent between devices are 32-bit elements; how exact they have to be, the bound alone decides.
No kernel may reach another device: no remote copies, remote signals or barrier semaphores. Data moves between devices by JAX's collectives and lax.ppermute only.
A program may use at most 64 MiB of HBM per device.

v0:
```python
import math

import jax
import jax.numpy as jnp
import numpy as np
from jax import lax
from jax.experimental import pallas as pl
from jax.experimental.pallas import tpu as pltpu
from jax.sharding import PartitionSpec as P

ORDER = 8
COEFFS = 512
CELLS = 32
LEAVES = 256
SLOTS = 16
OPERATORS = 8
NEAR_LEAVES = 6
LEVELS = 6
RIM = 8
LANES = 128
HALF = 64

F32, BF16 = jnp.float32, jnp.bfloat16


def cheb_value(k, x):
    previous, current = 1.0, x
    if k == 0:
        return previous
    for _ in range(k - 1):
        previous, current = current, 2.0 * x * current - previous
    return current


NODES = [math.cos((2 * m + 1) * math.pi / (2 * ORDER)) for m in range(ORDER)]
FACTORS = [
    [(1.0 if k == 0 else 2.0) / ORDER * cheb_value(k, NODES[m]) for m in range(ORDER)]
    for k in range(ORDER)
]


def child_map(side):
    shift = 2 * side - 1
    return np.array(
        [
            [
                sum(FACTORS[k][m] * cheb_value(k, (x + shift) / 2) for k in range(ORDER))
                for x in NODES
            ]
            for m in range(ORDER)
        ]
    )


MAPS = [child_map(0), child_map(1)]


def tile_maps(axis):
    eye = np.eye(ORDER)
    halves = []
    for matrix in MAPS:
        inner = np.kron(matrix, eye) if axis == 1 else np.kron(eye, matrix)
        halves.append(np.kron(np.eye(2), inner).T)
    whole = np.concatenate(halves, axis=0).astype(np.float32)
    high = whole.astype(jnp.bfloat16)
    low = (whole - high.astype(np.float32)).astype(jnp.bfloat16)
    return jnp.asarray(high), jnp.asarray(low)


def split(x):
    high = x.astype(BF16)
    return high, (x - high.astype(F32)).astype(BF16)


def mm(a, b, dims=((1,), (0,))):
    return lax.dot_general(a, b, (dims, ((), ())), preferred_element_type=F32)


def iota(shape, dim):
    return lax.broadcasted_iota(jnp.int32, shape, dim)


def map_outer(first, second):
    lower = iota((CELLS, LANES), 1) < HALF
    tiles = [first, second]
    turned = [[pltpu.roll(t, HALF, 1) for t in side] for side in tiles]
    result = []
    for i in range(4):
        total = None
        for s in range(2):
            for j in range(4):
                a = MAPS[s]
                same = jnp.where(lower, float(a[2 * i, 2 * j]), float(a[2 * i + 1, 2 * j + 1]))
                cross = jnp.where(lower, float(a[2 * i, 2 * j + 1]), float(a[2 * i + 1, 2 * j]))
                term = same * tiles[s][j] + cross * turned[s][j]
                total = term if total is None else total + term
        result.append(total)
    return result


def map_inner(pairs, high, low):
    rows = jnp.concatenate(
        [
            jnp.concatenate([first[j], second[j]], axis=1)
            for first, second in pairs
            for j in range(4)
        ],
        axis=0,
    )
    top, rest = split(rows)
    out = mm(top, high) + (mm(rest, high) + mm(top, low))
    return [
        [out[(t * 4 + j) * CELLS : (t * 4 + j + 1) * CELLS] for j in range(4)]
        for t in range(len(pairs))
    ]


def tiles_of(ref, i):
    return [ref[i, :, j * LANES : (j + 1) * LANES] for j in range(4)]


def put(ref, i, tiles):
    for j in range(4):
        ref[i, :, j * LANES : (j + 1) * LANES] = tiles[j]


def p2m_kernel(*refs):
    inputs = (len(refs) - 9) // 2
    fetched, refs = refs[:inputs], refs[inputs:]
    block, q, wz, first_half, last_half = refs[:5]
    landed, (wx_rows, strong, multipoles, done) = refs[5:-4], refs[-4:]
    copies = [
        pltpu.make_async_copy(source, target, done.at[i])
        for i, (source, target) in enumerate(zip(fetched, landed, strict=True))
    ]
    for copy in copies:
        copy.start()
    part, counts = landed[:2]
    shape = (ORDER, LEAVES)
    lane, node = iota(shape, 1), iota(shape, 0)
    shifts = [
        jnp.where((lane >> bit) & 1 == 1, 0.5, -0.5).astype(F32) for bit in (2, 1, 0)
    ]
    factors = []
    for k in range(1, ORDER):
        column = jnp.full(shape, FACTORS[k][0], F32)
        for m in range(1, ORDER):
            column = jnp.where(node == m, FACTORS[k][m], column)
        factors.append(column)

    def weights(row, shift):
        u = row * 0.5 + shift
        twice = u + u
        previous, current = jnp.ones(shape, F32), u
        total = factors[0] * u + 1.0 / ORDER
        for k in range(2, ORDER):
            previous, current = current, twice * current - previous
            total = total + factors[k - 1] * current
        return total

    for copy in copies[:2]:
        copy.wait()

    def slot(p, _):
        live = jnp.where(p < counts[...], 1.0, 0.0).astype(F32)
        strength = part[3, p] * live
        wx_rows[...] = weights(part[0, p], shifts[0])
        wy = weights(part[1, p], shifts[1])
        w = weights(part[2, p], shifts[2])
        wz[p] = w
        strong[p] = w * strength
        for a in range(ORDER):
            q[p, a] = wx_rows[a : a + 1, :] * wy
        for d in range(4):
            row = strength if d == 3 else part[d, p]
            first_half[d, pl.ds(p, 1), :] = row[:, :LANES]
            last_half[d, pl.ds(p, 1), :] = row[:, LANES:]
        return 0

    lax.fori_loop(0, SLOTS, slot, 0)
    for g in range(LEAVES // LANES):
        here = slice(g * LANES, (g + 1) * LANES)
        held = [strong[p, :, here] for p in range(SLOTS)]

        def outer(a, _):
            for b in range(ORDER):
                total = q[0, a, b : b + 1, here] * held[0]
                for p in range(1, SLOTS):
                    total = total + q[p, a, b : b + 1, here] * held[p]
                multipoles[a, b, :, here] = total
            return 0

        lax.fori_loop(0, ORDER, outer, 0)
    member = (iota((CELLS, LEAVES), 1) >> 3 == iota((CELLS, LEAVES), 0)).astype(F32).astype(BF16)
    high, low = split(multipoles[...].reshape(COEFFS, LEAVES))
    nt = ((1,), (1,))
    total = mm(member, high, nt) + mm(member, low, nt)
    for i in range(4):
        block[i] = total
    for copy in copies[2:]:
        copy.wait()


def own_place(level):
    return (lax.axis_index("leaf") >> level) & 3


def merge_low_kernel(got, high, low, before, after, group, sources):
    mine = own_place(0)
    pairs = [map_outer(tiles_of(got, 2 * t), tiles_of(got, 2 * t + 1)) for t in range(2)]
    merged = map_inner([pairs], high[...], low[...])[0]
    for i in range(4):
        put(group, i, merged)
    sources[0] = got[mine ^ 1]
    upper = mine >= 2
    put(sources, 1, [jnp.where(upper, pairs[0][j], pairs[1][j]) for j in range(4)])


def merge_mid_kernel(got, high, low, near, group, sources):
    mine = own_place(2)
    pairs = map_inner(
        [(tiles_of(got, 2 * t), tiles_of(got, 2 * t + 1)) for t in range(2)], high[...], low[...]
    )
    merged = map_outer(pairs[0], pairs[1])
    for i in range(4):
        put(group, i, merged)
    sources[0] = got[mine ^ 1]
    upper = mine >= 2
    put(sources, 1, [jnp.where(upper, pairs[0][j], pairs[1][j]) for j in range(4)])


def near_kernel(mine_first, mine_last, before, after, lists, near, sources):
    lane = iota((8, LANES), 1)
    for g in range(2):
        here = slice(g * LANES, (g + 1) * LANES)
        own = (mine_first, mine_last)[g]

        for t in range(NEAR_LEAVES):
            leaf = lists[t, :, here] - RIM
            place = jnp.broadcast_to(leaf & (LANES - 1), (8, LANES))
            inside = jnp.broadcast_to(leaf >> 7, (8, LANES)) == g
            for d in range(4):
                for half in range(2):
                    rows = slice(half * 8, half * 8 + 8)
                    middle = own[d, rows, :]
                    if g == 0:
                        edge = jnp.where(lane < HALF, mine_last[d, rows, :], before[d, rows, :])
                    else:
                        edge = jnp.where(lane < HALF, after[d, rows, :], mine_first[d, rows, :])
                    sources[t, d, rows, :] = jnp.where(
                        inside,
                        jnp.take_along_axis(middle, place, axis=1, mode="promise_in_bounds"),
                        jnp.take_along_axis(edge, place, axis=1, mode="promise_in_bounds"),
                    )
        target = [own[d] for d in range(3)]

        def pair(t, total):
            for s in range(SLOTS):
                dist = None
                for d in range(3):
                    offset = target[d] - sources[t, d, s : s + 1, :]
                    dist = offset * offset if dist is None else dist + offset * offset
                total = total + lax.rsqrt(dist + 1.0) * sources[t, 3, s : s + 1, :]
            return total

        near[:, here] = lax.fori_loop(0, NEAR_LEAVES, pair, jnp.zeros((SLOTS, LANES), F32))


def select_kernel(pattern, block, low_sources, mid_sources, select, gathered, codes, stack):
    codes[...] = jnp.zeros(codes.shape, jnp.int32)
    for v in range(LEVELS + 1):
        codes[:, v * CELLS : (v + 1) * CELLS] = pattern[v]
    for o in range(OPERATORS):
        rows = slice(o * CELLS, (o + 1) * CELLS)
        select[rows, :] = (codes[...] == o + 1).astype(F32).astype(BF16)
    stack[0:CELLS] = block[0]
    for i in range(2):
        stack[(1 + i) * CELLS : (2 + i) * CELLS] = low_sources[i]
        stack[(3 + i) * CELLS : (4 + i) * CELLS] = mid_sources[i]
    high, low = split(stack[...])
    known = select[:, : 5 * CELLS]
    gathered[...] = mm(known, high) + mm(known, low)


def final_kernel(kernels, got, high, low, select, gathered, q, wz, near, counts, *rest):
    potential, local_exp, stack, leaf_local, operators, done = rest
    copies = [
        pltpu.make_async_copy(kernels.at[o], operators.at[o], done.at[o]) for o in range(OPERATORS)
    ]
    for copy in copies:
        copy.start()
    mine = own_place(4)
    stack[0:CELLS] = got[mine ^ 1]
    other = (mine ^ 2) & 2
    merged = map_inner(
        [(tiles_of(got, other), tiles_of(got, other + 1))], high[...], low[...]
    )[0]
    for j in range(4):
        stack[CELLS:, j * LANES : (j + 1) * LANES] = merged[j]
    top, rest = split(stack[...])
    last = select[:, 5 * CELLS : 7 * CELLS]
    top, rest = split(gathered[...] + (mm(last, top) + mm(last, rest)))
    total = None
    for o in range(OPERATORS):
        rows = slice(o * CELLS, (o + 1) * CELLS)
        both = jnp.concatenate([top[rows], rest[rows]], axis=0)
        copies[o].wait()
        term = mm(both, operators[o])
        total = term if total is None else total + term
    cells = total[:CELLS] + total[CELLS:]
    local_exp[...] = cells
    member = (iota((CELLS, LEAVES), 1) >> 3 == iota((CELLS, LEAVES), 0)).astype(F32).astype(BF16)
    top, rest = split(cells)
    tn = ((0,), (0,))
    leaf_local[...] = (mm(top, member, tn) + mm(rest, member, tn)).reshape(leaf_local.shape)
    for g in range(LEAVES // LANES):
        here = slice(g * LANES, (g + 1) * LANES)

        def outer(a, totals):
            totals = list(totals)
            for b in range(ORDER):
                piece = leaf_local[a, b, :, here]
                for p in range(SLOTS):
                    totals[p] = totals[p] + q[p, a, b : b + 1, here] * piece
            return tuple(totals)

        zero = jnp.zeros((ORDER, LANES), F32)
        totals = lax.fori_loop(0, ORDER, outer, (zero,) * SLOTS)
        for p in range(SLOTS):
            far = jnp.sum(totals[p] * wz[p, :, here], axis=0, keepdims=True)
            live = jnp.where(p < counts[:, here], 1.0, 0.0).astype(F32)
            potential[p, :, here] = (far + near[p : p + 1, here]) * live


def held(*values, space=pltpu.VMEM):
    return [pltpu.with_memory_space_constraint(v, space) for v in values]


def call(kernel, outs, args, scratch=(), cost=(0, 0), remote=()):
    whole = pl.BlockSpec(memory_space=pltpu.VMEM)
    return pl.pallas_call(
        kernel,
        out_shape=outs,
        in_specs=[pl.BlockSpec(memory_space=pltpu.HBM)] * len(remote) + [whole] * len(args),
        scratch_shapes=list(scratch),
        cost_estimate=pl.CostEstimate(flops=cost[0], bytes_accessed=cost[1], transcendentals=0),
        compiler_params=pltpu.CompilerParams(vmem_limit_bytes=8 << 20),
    )(*held(*remote, space=pltpu.HBM), *held(*args))


def exchange(group, level, steps, count):
    groups, seen = [], set()
    for i in range(count):
        if i in seen:
            continue
        members = [i, i ^ steps[0], i ^ steps[1], i ^ steps[0] ^ steps[1]]
        members.sort(key=lambda l: (l >> level) & 3)
        seen.update(members)
        groups.append(members)
    return lax.all_to_all(group, "leaf", 0, 0, axis_index_groups=groups)


def local(particles, counts, neighbours, pattern, kernels):
    vmem = pltpu.VMEM
    block_shape = (4, CELLS, COEFFS)
    pair_shape = (2, CELLS, COEFFS)
    count = lax.axis_size("leaf")
    q_shape = (SLOTS, ORDER, ORDER, LEAVES)
    w_shape = (SLOTS, ORDER, LEAVES)
    inputs = (particles, counts, neighbours.transpose(1, 0, 2), pattern[0], *tile_maps(1), *tile_maps(2))
    block, q, wz, first_half, last_half, *landed = call(
        p2m_kernel,
        (
            vmem(block_shape, F32),
            vmem(q_shape, F32),
            vmem(w_shape, F32),
            vmem((4, SLOTS, LANES), F32),
            vmem((4, SLOTS, LANES), F32),
            *[vmem(x.shape, x.dtype) for x in inputs],
        ),
        (),
        (
            vmem((ORDER, LEAVES), F32),
            vmem(w_shape, F32),
            vmem((ORDER,) * 3 + (LEAVES,), F32),
            pltpu.SemaphoreType.DMA((len(inputs),)),
        ),
        (10_000_000, 2_000_000),
        inputs,
    )
    counts, neighbours, pattern = landed[1:4]
    mid_maps, inner_maps = landed[4:6], landed[6:8]
    got = exchange(block, 0, (1, 2), count)
    width = lax.axis_size("near")
    forward = [(i, i + 1) for i in range(width - 1)]
    before = lax.ppermute(last_half, "near", forward)
    after = lax.ppermute(first_half, "near", [(t, s) for s, t in forward])
    group, low_sources = call(
        merge_low_kernel,
        (vmem(block_shape, F32), vmem(pair_shape, F32)),
        (got, *mid_maps, before, after),
        cost=(1_000_000, 1_000_000),
    )
    got = exchange(group, 2, (7, 8), count)
    near = call(
        near_kernel,
        vmem((SLOTS, LEAVES), F32),
        (first_half, last_half, before, after, neighbours),
        (vmem((NEAR_LEAVES, 4, SLOTS, LANES), F32),),
        (2_000_000_000, 8_000_000),
    )
    group, mid_sources = call(
        merge_mid_kernel,
        (vmem(block_shape, F32), vmem(pair_shape, F32)),
        (got, *inner_maps, near),
        cost=(1_000_000, 1_000_000),
    )
    got = exchange(group, 4, (16, 56), count)
    select, gathered = call(
        select_kernel,
        (vmem((256, 256), BF16), vmem((256, COEFFS), F32)),
        (pattern, block, low_sources, mid_sources),
        (vmem((CELLS, 256), jnp.int32), vmem((5 * CELLS, COEFFS), F32)),
        (1_000_000_000, 8_000_000),
    )
    potential, local_exp = call(
        final_kernel,
        (
            jax.ShapeDtypeStruct((SLOTS, 1, LEAVES), F32),
            jax.ShapeDtypeStruct((CELLS, COEFFS), F32),
        ),
        (got, *mid_maps, select, gathered, q, wz, near, counts),
        (
            vmem((2 * CELLS, COEFFS), F32),
            vmem((ORDER,) * 3 + (LEAVES,), F32),
            vmem(kernels.shape, BF16),
            pltpu.SemaphoreType.DMA((OPERATORS,)),
        ),
        (1_000_000_000, 8_000_000),
        (kernels,),
    )
    return potential, local_exp[None]


def solution(mesh):
    placed = (
        P(None, None, "leaf", "near"),
        P("leaf", "near"),
        P("leaf", None, "near"),
        P("leaf", None, None, "near"),
        P(),
    )
    return jax.shard_map(
        local,
        mesh=mesh,
        in_specs=placed,
        out_specs=(P(None, "leaf", "near"), P("leaf", "near", None)),
        check_vma=False,
    )
```

profile of v0, /device:TPU:4, one launch (start us, length us, event | category | flops | bytes accessed | tf_op | source)
XLA Modules:
  0.0 61.0 jit_solution(8972012237265352960)
XLA Ops:
  0.6 3.2 %shard_map.104 = (f32[4,32,512]{2,1,0:T(8,128)}, f32[16,8,8,256]{3,2,1,0:T(8,128)S(1)}, f32[16,8,256]{2,1,0:T(8,128)S(1)}, f32[4,16,128]{2,1,0:T(8,128)S(1)}, f3...) custom-call(f32[4,16,1,256]{3,2,1,0:T(1,128)} %refs_0_.1, ...), custom_call_target="tpu_custom_call" | custom-call | flops 10000000 | bytes 2000000 | tf_op jit(solution)/shard_map/pallas_call | solution.py:341
  3.9 7.3 %all-to-all-start = ((f32[4,32,512]{2,1,0:T(8,128)}), f32[4,32,512]{2,1,0:T(8,128)S(1)}, u32[]{:S(2)}, u32[]{:S(2)}) async-start(f32[4,32,512]{2,1,0:T(8,128)} %get-tuple-element.22.block), calls=%async_computation | async-start | bytes 524288 | tf_op jit(solution)/shard_map/all_to_all | solution.py:360
  11.1 1.9 %collective-permute-start = (f32[4,16,128]{2,1,0:T(8,128)S(1)}, f32[4,16,128]{2,1,0:T(8,128)S(1)}, u32[]{:S(2)}, u32[]{:S(2)}) collective-permute-start(f32[4,16,128]{2,1,0:T(8,128)S(1)} %get-tuple-element.25.mine_last), channel_id=1, source_target_pairs={{0,1},{1,2},{2,3},{3,4},{4,5},{5,6},{6,7},{8,9},{9,10},{10,11},{11... | collective-permute-start | bytes 98312 | tf_op jit(solution)/shard_map/ppermute | solution.py:396
  13.1 3.6 %collective-permute-start.1 = (f32[4,16,128]{2,1,0:T(8,128)S(1)}, f32[4,16,128]{2,1,0:T(8,128)S(1)}, u32[]{:S(2)}, u32[]{:S(2)}) collective-permute-start(f32[4,16,128]{2,1,0:T(8,128)S(1)} %get-tuple-element.26.mine_first), channel_id=1, source_target_pairs={{1,0},{2,1},{3,2},{4,3},{5,4},{6,5},{7,6},{9,8},{10,9},{11,10},{12... | collective-permute-start | bytes 98312 | tf_op jit(solution)/shard_map/ppermute | solution.py:397
  16.7 0.0 collective-permute-done.before
  16.7 1.6 %collective-permute-done.1.after = f32[4,16,128]{2,1,0:T(8,128)S(1)} collective-permute-done((f32[4,16,128]{2,1,0:T(8,128)S(1)}, f32[4,16,128]{2,1,0:T(8,128)S(1)}, u32[]{:S(2)}, u32[]{:S(2)}) %collective-permute-start.1) | collective-permute-done | bytes 32800 | tf_op jit(solution)/shard_map/ppermute | solution.py:397
  18.3 1.8 %all-to-all-done.got = f32[4,32,512]{2,1,0:T(8,128)S(1)} async-done(((f32[4,32,512]{2,1,0:T(8,128)}), f32[4,32,512]{2,1,0:T(8,128)S(1)}, u32[]{:S(2)}, u32[]{:S(2)}) %all-to-all-start) | async-done | bytes 262176 | tf_op jit(solution)/shard_map/all_to_all | solution.py:360
  20.1 1.1 %shard_map.105 = (f32[4,32,512]{2,1,0:T(8,128)}, f32[2,32,512]{2,1,0:T(8,128)S(1)}) custom-call(f32[4,32,512]{2,1,0:T(8,128)S(1)} %all-to-all-done.got, bf16[256,128]{1,0:T(8,128)(2,1)S(1)} %get-tuple-element.23.high, bf16[256,128]{1,0:T(8,128)(2,1)S(1)} %get-tuple-element.24.low, f32[4,16,128]{2,1,0:T(8,128)S(1)} %collective-permute-done.before, ...), custom_call_target="tpu_custom_call" | custom-call | flops 1000000 | bytes 1000000 | tf_op jit(solution)/shard_map/pallas_call | solution.py:341
  21.2 7.4 %all-to-all-start.1 = ((f32[4,32,512]{2,1,0:T(8,128)}), f32[4,32,512]{2,1,0:T(8,128)S(1)}, u32[]{:S(2)}, u32[]{:S(2)}) async-start(f32[4,32,512]{2,1,0:T(8,128)} %get-tuple-element.27), calls=%async_computation.1 | async-start | bytes 524288 | tf_op jit(solution)/shard_map/all_to_all | solution.py:360
  28.5 1.1 %shard_map.106.near = f32[16,256]{1,0:T(8,128)S(1)} custom-call(f32[4,16,128]{2,1,0:T(8,128)S(1)} %get-tuple-element.26.mine_first, f32[4,16,128]{2,1,0:T(8,128)S(1)} %get-tuple-element.25.mine_last, f32[4,16,128]{2,1,0:T(8,128)S(1)} %collective-permute-done.before, f32[4,16,128]{2,1,0:T(8,128)S(1)} %collective-permute-done.1.after, ...), custom_call_target="tpu_custom_call" | custom-call | flops 2000000000 | bytes 8000000 | tf_op jit(solution)/shard_map/pallas_call | solution.py:341
  29.6 9.4 %all-to-all-done.1.got = f32[4,32,512]{2,1,0:T(8,128)S(1)} async-done(((f32[4,32,512]{2,1,0:T(8,128)}), f32[4,32,512]{2,1,0:T(8,128)S(1)}, u32[]{:S(2)}, u32[]{:S(2)}) %all-to-all-start.1) | async-done | bytes 262176 | tf_op jit(solution)/shard_map/all_to_all | solution.py:360
  39.1 1.0 %shard_map.107 = (f32[4,32,512]{2,1,0:T(8,128)}, f32[2,32,512]{2,1,0:T(8,128)S(1)}) custom-call(f32[4,32,512]{2,1,0:T(8,128)S(1)} %all-to-all-done.1.got, bf16[256,128]{1,0:T(8,128)(2,1)S(1)} %get-tuple-element.28.high, bf16[256,128]{1,0:T(8,128)(2,1)S(1)} %get-tuple-element.29.low, f32[16,256]{1,0:T(8,128)S(1)} %shard_map.106.near), custom_call_target="tpu_custom_call" | custom-call | flops 1000000 | bytes 1000000 | tf_op jit(solution)/shard_map/pallas_call | solution.py:341
  40.1 6.2 %all-to-all-start.2 = ((f32[4,32,512]{2,1,0:T(8,128)}), f32[4,32,512]{2,1,0:T(8,128)S(1)}, u32[]{:S(2)}, u32[]{:S(2)}) async-start(f32[4,32,512]{2,1,0:T(8,128)} %get-tuple-element.31), calls=%async_computation.2 | async-start | bytes 524288 | tf_op jit(solution)/shard_map/all_to_all | solution.py:360
  46.4 1.3 %shard_map.108 = (bf16[256,256]{1,0:T(8,128)(2,1)S(1)}, f32[256,512]{1,0:T(8,128)S(1)}) custom-call(s32[7,32,32]{2,1,0:T(8,128)S(1)} %get-tuple-element.32.pattern, f32[4,32,512]{2,1,0:T(8,128)} %get-tuple-element.22.block, f32[2,32,512]{2,1,0:T(8,128)S(1)} %get-tuple-element.33.low_sources, f32[2,32,512]{2,1,0:T(8,128)S(1)} %get-tuple-element.34.mid_sources), custom_call_target="tpu_custom_call" | custom-call | flops 1000000000 | bytes 8000000 | tf_op jit(solution)/shard_map/pallas_call | solution.py:341
  47.7 9.2 %all-to-all-done.2.got = f32[4,32,512]{2,1,0:T(8,128)S(1)} async-done(((f32[4,32,512]{2,1,0:T(8,128)}), f32[4,32,512]{2,1,0:T(8,128)S(1)}, u32[]{:S(2)}, u32[]{:S(2)}) %all-to-all-start.2) | async-done | bytes 262176 | tf_op jit(solution)/shard_map/all_to_all | solution.py:360
  56.9 4.1 %shard_map.109 = (f32[16,1,256]{2,1,0:T(1,128)}, f32[32,512]{1,0:T(8,128)}) custom-call(bf16[8,512,512]{2,1,0:T(8,128)(2,1)} %kernels.1, f32[4,32,512]{2,1,0:T(8,128)S(1)} %all-to-all-done.2.got, bf16[256,128]{1,0:T(8,128)(2,1)S(1)} %get-tuple-element.23.high, bf16[256,128]{1,0:T(8,128)(2,1)S(1)} %get-tuple-element.24.low, ...), custom_call_target="tpu_custom_call" | custom-call | flops 1000000000 | bytes 8000000 | tf_op jit(solution)/shard_map/pallas_call | solution.py:341
Async XLA Ops:
  3.9 16.2 %all-to-all-start = ((f32[4,32,512]{2,1,0:T(8,128)}), f32[4,32,512]{2,1,0:T(8,128)S(1)}, u32[]{:S(2)}, u32[]{:S(2)}) async-start(f32[4,32,512]{2,1,0:T(8,128)} %get-tuple-element.22.block), calls=%async_computation | async-start | bytes 524288 | tf_op jit(solution)/shard_map/all_to_all | solution.py:360
  11.1 5.6 %collective-permute-start = (f32[4,16,128]{2,1,0:T(8,128)S(1)}, f32[4,16,128]{2,1,0:T(8,128)S(1)}, u32[]{:S(2)}, u32[]{:S(2)}) collective-permute-start(f32[4,16,128]{2,1,0:T(8,128)S(1)} %get-tuple-element.25.mine_last), channel_id=1, source_target_pairs={{0,1},{1,2},{2,3},{3,4},{4,5},{5,6},{6,7},{8,9},{9,10},{10,11},{11... | collective-permute-start | bytes 98312 | tf_op jit(solution)/shard_map/ppermute | solution.py:396
  13.1 5.2 %collective-permute-start.1 = (f32[4,16,128]{2,1,0:T(8,128)S(1)}, f32[4,16,128]{2,1,0:T(8,128)S(1)}, u32[]{:S(2)}, u32[]{:S(2)}) collective-permute-start(f32[4,16,128]{2,1,0:T(8,128)S(1)} %get-tuple-element.26.mine_first), channel_id=1, source_target_pairs={{1,0},{2,1},{3,2},{4,3},{5,4},{6,5},{7,6},{9,8},{10,9},{11,10},{12... | collective-permute-start | bytes 98312 | tf_op jit(solution)/shard_map/ppermute | solution.py:397
  21.2 17.9 %all-to-all-start.1 = ((f32[4,32,512]{2,1,0:T(8,128)}), f32[4,32,512]{2,1,0:T(8,128)S(1)}, u32[]{:S(2)}, u32[]{:S(2)}) async-start(f32[4,32,512]{2,1,0:T(8,128)} %get-tuple-element.27), calls=%async_computation.1 | async-start | bytes 524288 | tf_op jit(solution)/shard_map/all_to_all | solution.py:360
  40.1 16.8 %all-to-all-start.2 = ((f32[4,32,512]{2,1,0:T(8,128)}), f32[4,32,512]{2,1,0:T(8,128)S(1)}, u32[]{:S(2)}, u32[]{:S(2)}) async-start(f32[4,32,512]{2,1,0:T(8,128)} %get-tuple-element.31), calls=%async_computation.2 | async-start | bytes 524288 | tf_op jit(solution)/shard_map/all_to_all | solution.py:360
where the time goes:
time: 61.5 us; the launch traced here: 61 us
  starting transfers between devices  26.5 us (43%)
  waiting for transfers between devices  22 us (36%)
  Pallas kernels  11.9 us (19%)
  between operations  0.68 us (1%)
    all_to_all x3, starting transfers between devices, exchange(): return lax.all_to_all(group, 'leaf', 0, 0, axis_index_groups=groups)  20.9 us
    all_to_all x3, waiting for transfers between devices, exchange(): return lax.all_to_all(group, 'leaf', 0, 0, axis_index_groups=groups)  20.4 us
    pallas_call x6, Pallas kernels, call(): pl.pallas_call(kernel, out_shape=outs, in_specs=[pl.BlockSpec(memory_spac...  11.9 us
    ppermute x1, starting transfers between devices, local(): after = lax.ppermute(first_half, 'near', [(t, s) for s, t in forward])  3.64 us
    ppermute x1, starting transfers between devices, local(): before = lax.ppermute(last_half, 'near', forward)  1.91 us
    ppermute x1, waiting for transfers between devices, local(): after = lax.ppermute(first_half, 'near', [(t, s) for s, t in forward])  1.57 us
  transfers between devices with their start and end apart: 5, of which 4 were waited for; matrix products, arithmetic and copies ran while one was open for 0% of the time, Pallas kernels for 4%

commit v1 on v0

v1 whole, which is shorter than its diff:
```python
import math

import jax
import jax.numpy as jnp
import numpy as np
from jax import lax
from jax.experimental import pallas as pl
from jax.experimental.pallas import tpu as pltpu
from jax.sharding import PartitionSpec as P

ORDER = 8
COEFFS = 512
CELLS = 32
LEAVES = 256
SLOTS = 16
OPERATORS = 8
NEAR_LEAVES = 6
LEVELS = 6
RIM = 8
LANES = 128
HALF = 64
AHEAD = 2

F32, BF16 = jnp.float32, jnp.bfloat16


def cheb_value(k, x):
    previous, current = 1.0, x
    if k == 0:
        return previous
    for _ in range(k - 1):
        previous, current = current, 2.0 * x * current - previous
    return current


NODES = [math.cos((2 * m + 1) * math.pi / (2 * ORDER)) for m in range(ORDER)]
FACTORS = [
    [(1.0 if k == 0 else 2.0) / ORDER * cheb_value(k, NODES[m]) for m in range(ORDER)]
    for k in range(ORDER)
]


def child_map(side):
    shift = 2 * side - 1
    return np.array(
        [
            [
                sum(FACTORS[k][m] * cheb_value(k, (x + shift) / 2) for k in range(ORDER))
                for x in NODES
            ]
            for m in range(ORDER)
        ]
    )


MAPS = [child_map(0), child_map(1)]


def tile_maps(axis):
    eye = np.eye(ORDER)
    halves = []
    for matrix in MAPS:
        inner = np.kron(matrix, eye) if axis == 1 else np.kron(eye, matrix)
        halves.append(np.kron(np.eye(2), inner).T)
    whole = np.concatenate(halves, axis=0).astype(np.float32)
    high = whole.astype(jnp.bfloat16)
    low = (whole - high.astype(np.float32)).astype(jnp.bfloat16)
    return jnp.asarray(high), jnp.asarray(low)


def split(x):
    high = x.astype(BF16)
    return high, (x - high.astype(F32)).astype(BF16)


def mm(a, b, dims=((1,), (0,))):
    return lax.dot_general(a, b, (dims, ((), ())), preferred_element_type=F32)


def iota(shape, dim):
    return lax.broadcasted_iota(jnp.int32, shape, dim)


def map_outer(first, second):
    lower = iota((CELLS, LANES), 1) < HALF
    tiles = [first, second]
    turned = [[pltpu.roll(t, HALF, 1) for t in side] for side in tiles]
    result = []
    for i in range(4):
        total = None
        for s in range(2):
            for j in range(4):
                a = MAPS[s]
                same = jnp.where(lower, float(a[2 * i, 2 * j]), float(a[2 * i + 1, 2 * j + 1]))
                cross = jnp.where(lower, float(a[2 * i, 2 * j + 1]), float(a[2 * i + 1, 2 * j]))
                term = same * tiles[s][j] + cross * turned[s][j]
                total = term if total is None else total + term
        result.append(total)
    return result


def map_inner(pairs, high, low):
    rows = jnp.concatenate(
        [
            jnp.concatenate([first[j], second[j]], axis=1)
            for first, second in pairs
            for j in range(4)
        ],
        axis=0,
    )
    top, rest = split(rows)
    out = mm(top, high) + (mm(rest, high) + mm(top, low))
    return [
        [out[(t * 4 + j) * CELLS : (t * 4 + j + 1) * CELLS] for j in range(4)]
        for t in range(len(pairs))
    ]


def tiles_of(ref, i):
    return [ref[i, :, j * LANES : (j + 1) * LANES] for j in range(4)]


def put(ref, tiles):
    for j in range(4):
        ref[:, j * LANES : (j + 1) * LANES] = tiles[j]


def put_sources(sources, got, pairs, mine):
    sources[0] = got[mine ^ 1]
    upper = mine >= 2
    put(sources.at[1], [jnp.where(upper, pairs[0][j], pairs[1][j]) for j in range(4)])


def send_all(block, group, done):
    copies = [pltpu.make_async_copy(block, group.at[i], done.at[i]) for i in range(4)]
    for copy in copies:
        copy.start()
    return copies


def dense_weights(u):
    terms = [None, u, 2.0 * u * u - 1.0]
    twice = u + u
    for _ in range(3, ORDER):
        terms.append(twice * terms[-1] - terms[-2])
    weights = [None] * ORDER
    for m in range(ORDER // 2):
        even = FACTORS[0][m] + FACTORS[2][m] * terms[2]
        odd = FACTORS[1][m] * u
        for k in range(3, ORDER):
            if k % 2:
                odd = odd + FACTORS[k][m] * terms[k]
            else:
                even = even + FACTORS[k][m] * terms[k]
        weights[m] = even + odd
        weights[ORDER - 1 - m] = even - odd
    return weights


def p2m_kernel(*refs):
    inputs = (len(refs) - 9) // 2
    fetched, refs = refs[:inputs], refs[inputs:]
    block, wx, wy, wz, dense = refs[:5]
    landed, (rows, strong, multipoles, done) = refs[5:-4], refs[-4:]
    copies = [
        pltpu.make_async_copy(source, target, done.at[i])
        for i, (source, target) in enumerate(zip(fetched, landed, strict=True))
    ]
    for copy in copies:
        copy.start()
    for copy in copies[:2]:
        copy.wait()
    part, counts = landed[:2]
    for d in range(4):
        for p in range(SLOTS):
            dense[d, p : p + 1, :] = part[d, p]
    shape = (SLOTS, LEAVES)
    dense[3] = dense[3] * (iota(shape, 0) < counts[...]).astype(F32)
    lane = iota(shape, 1)
    for d, bit in enumerate((2, 1, 0)):
        shift = jnp.where((lane >> bit) & 1 == 1, 0.5, -0.5).astype(F32)
        for m, weight in enumerate(dense_weights(dense[d] * 0.5 + shift)):
            if d == 2:
                for g in range(2):
                    at = (g * ORDER + m) * SLOTS
                    rows[at : at + SLOTS, :] = weight[:, g * LANES : (g + 1) * LANES]
            else:
                (wx, wy)[d][m] = weight
    for p in range(SLOTS):
        for g in range(LEAVES // LANES):
            here = slice(g * LANES, (g + 1) * LANES)
            w = rows[pl.ds(g * ORDER * SLOTS + p, ORDER, stride=SLOTS), :]
            wz[p, :, here] = w
            w = w * dense[3, p : p + 1, here]
            for b in range(ORDER):
                strong[p, b, :, here] = w * wy[b, p : p + 1, here]
    for g in range(LEAVES // LANES):
        here = slice(g * LANES, (g + 1) * LANES)
        for start in range(0, ORDER, 4):
            totals = [[None] * ORDER for _ in range(4)]
            for p in range(SLOTS):
                pieces = [strong[p, b, :, here] for b in range(ORDER)]
                for a in range(4):
                    weight = wx[start + a, p : p + 1, here]
                    for b in range(ORDER):
                        term = weight * pieces[b]
                        totals[a][b] = term if p == 0 else totals[a][b] + term
            for a in range(4):
                for b in range(ORDER):
                    multipoles[start + a, b, :, here] = totals[a][b]
    member = (iota((CELLS, LEAVES), 1) >> 3 == iota((CELLS, LEAVES), 0)).astype(F32).astype(BF16)
    high, low = split(multipoles[...].reshape(COEFFS, LEAVES))
    nt = ((1,), (1,))
    block[...] = mm(member, high, nt) + mm(member, low, nt)
    for copy in copies[2:]:
        copy.wait()


def own_place(level):
    return (lax.axis_index("leaf") >> level) & 3


def merge_first_kernel(got, group, source):
    source[...] = got[1 - (own_place(0) & 1)]
    put(group, map_outer(tiles_of(got, 0), tiles_of(got, 1)))


def merge_second_kernel(got, high, low, dense, group, source, last_half, block, done):
    put(block, map_inner([(tiles_of(got, 0), tiles_of(got, 1))], high[...], low[...])[0])
    copies = send_all(block, group, done)
    source[...] = got[1 - (own_place(1) & 1)]
    last_half[...] = dense[:, :, LANES:]
    for copy in copies:
        copy.wait()


def merge_mid_kernel(got, high, low, dense, before, group, sources, first_half, block, done):
    mine = own_place(2)
    pairs = map_inner(
        [(tiles_of(got, 2 * t), tiles_of(got, 2 * t + 1)) for t in range(2)], high[...], low[...]
    )
    put(block, map_outer(pairs[0], pairs[1]))
    copies = send_all(block, group, done)
    first_half[...] = dense[:, :, :LANES]
    put_sources(sources, got, pairs, mine)
    for copy in copies:
        copy.wait()


def near_kernel(mine_first, mine_last, before, after, lists, near, sources):
    lane = iota((8, LANES), 1)
    for g in range(2):
        here = slice(g * LANES, (g + 1) * LANES)
        own = (mine_first, mine_last)[g]

        for t in range(NEAR_LEAVES):
            leaf = lists[t, :, here] - RIM
            place = jnp.broadcast_to(leaf & (LANES - 1), (8, LANES))
            inside = jnp.broadcast_to(leaf >> 7, (8, LANES)) == g
            for d in range(4):
                for half in range(2):
                    rows = slice(half * 8, half * 8 + 8)
                    middle = own[d, rows, :]
                    if g == 0:
                        edge = jnp.where(lane < HALF, mine_last[d, rows, :], before[d, rows, :])
                    else:
                        edge = jnp.where(lane < HALF, after[d, rows, :], mine_first[d, rows, :])
                    sources[t, d, rows, :] = jnp.where(
                        inside,
                        jnp.take_along_axis(middle, place, axis=1, mode="promise_in_bounds"),
                        jnp.take_along_axis(edge, place, axis=1, mode="promise_in_bounds"),
                    )
        target = [own[d] for d in range(3)]

        def pair(t, total):
            for s in range(SLOTS):
                dist = None
                for d in range(3):
                    offset = target[d] - sources[t, d, s : s + 1, :]
                    dist = offset * offset if dist is None else dist + offset * offset
                total = total + lax.rsqrt(dist + 1.0) * sources[t, 3, s : s + 1, :]
            return total

        near[:, here] = lax.fori_loop(0, NEAR_LEAVES, pair, jnp.zeros((SLOTS, LANES), F32))


def select_kernel(kernels, pattern, block, first, second, mid_sources, select, gathered, fetched, codes, stack, done):
    copies = [
        pltpu.make_async_copy(kernels.at[o], fetched.at[o], done.at[o]) for o in range(AHEAD)
    ]
    for copy in copies:
        copy.start()
    codes[...] = jnp.zeros(codes.shape, jnp.int32)
    for v in range(LEVELS + 1):
        codes[:, v * CELLS : (v + 1) * CELLS] = pattern[v]
    for o in range(OPERATORS):
        rows = slice(o * CELLS, (o + 1) * CELLS)
        select[rows, :] = (codes[...] == o + 1).astype(F32).astype(BF16)
    stack[0:CELLS] = block[...]
    stack[CELLS : 2 * CELLS] = first[...]
    stack[2 * CELLS : 3 * CELLS] = second[...]
    for i in range(2):
        stack[(3 + i) * CELLS : (4 + i) * CELLS] = mid_sources[i]
    high, low = split(stack[...])
    known = select[:, : 5 * CELLS]
    gathered[...] = mm(known, high) + mm(known, low)
    for copy in copies:
        copy.wait()


def final_kernel(
    kernels, got, high, low, select, gathered, fetched, wx, wy, wz, near, counts,
    potential, local_exp, stack, leaf_local, operators, cells, values, done,
):
    copies = [
        pltpu.make_async_copy(kernels.at[AHEAD + o], operators.at[o], done.at[o])
        for o in range(OPERATORS - AHEAD)
    ]
    for copy in copies:
        copy.start()
    mine = own_place(4)
    stack[0:CELLS] = got[mine ^ 1]
    other = (mine ^ 2) & 2
    merged = map_inner(
        [(tiles_of(got, other), tiles_of(got, other + 1))], high[...], low[...]
    )[0]
    put(stack.at[CELLS:], merged)
    top, rest = split(stack[...])
    last = select[:, 5 * CELLS : 7 * CELLS]
    top, rest = split(gathered[...] + (mm(last, top) + mm(last, rest)))
    total = None
    for o in range(OPERATORS):
        rows = slice(o * CELLS, (o + 1) * CELLS)
        both = jnp.concatenate([top[rows], rest[rows]], axis=0)
        if o < AHEAD:
            operator = fetched[o]
        else:
            copies[o - AHEAD].wait()
            operator = operators[o - AHEAD]
        term = mm(both, operator)
        total = term if total is None else total + term
    total = total[:CELLS] + total[CELLS:]
    cells[...] = total
    outs = [pltpu.make_async_copy(cells, local_exp, done.at[OPERATORS])]
    outs[0].start()
    member = (iota((CELLS, LEAVES), 1) >> 3 == iota((CELLS, LEAVES), 0)).astype(F32).astype(BF16)
    top, rest = split(total)
    both = jnp.concatenate([top, rest], axis=0)
    twice = jnp.concatenate([member, member], axis=0)
    leaf_local[...] = mm(both, twice, ((0,), (0,))).reshape(leaf_local.shape)
    for g in range(LEAVES // LANES):
        here = slice(g * LANES, (g + 1) * LANES)
        for start in range(0, SLOTS, 4):
            slots = range(start, start + 4)
            depth = [wz[p, :, here] for p in slots]
            pieces = [
                [depth[i] * wy[b, p : p + 1, here] for b in range(ORDER)]
                for i, p in enumerate(slots)
            ]
            totals = [None] * 4
            for a in range(ORDER):
                inner = [None] * 4
                for b in range(ORDER):
                    tile = leaf_local[a, b, :, here]
                    for i in range(4):
                        term = pieces[i][b] * tile
                        inner[i] = term if b == 0 else inner[i] + term
                for i, p in enumerate(slots):
                    term = inner[i] * wx[a, p : p + 1, here]
                    totals[i] = term if a == 0 else totals[i] + term
            for i, p in enumerate(slots):
                far = jnp.sum(totals[i], axis=0, keepdims=True)
                live = jnp.where(p < counts[:, here], 1.0, 0.0).astype(F32)
                values[p, :, here] = (far + near[p : p + 1, here]) * live
        half = pltpu.make_async_copy(
            values.at[:, :, here], potential.at[:, :, here], done.at[OPERATORS - AHEAD + g]
        )
        half.start()
        outs.append(half)
    for out in outs:
        out.wait()


def held(*values, space=pltpu.VMEM):
    return [pltpu.with_memory_space_constraint(v, space) for v in values]


def call(kernel, outs, args, scratch=(), cost=(0, 0), remote=()):
    whole = pl.BlockSpec(memory_space=pltpu.VMEM)
    apart = pl.BlockSpec(memory_space=pltpu.HBM)
    return pl.pallas_call(
        kernel,
        out_shape=outs,
        in_specs=[apart] * len(remote) + [whole] * len(args),
        out_specs=[apart if o.memory_space == pltpu.HBM else whole for o in outs],
        scratch_shapes=list(scratch),
        cost_estimate=pl.CostEstimate(flops=cost[0], bytes_accessed=cost[1], transcendentals=0),
        compiler_params=pltpu.CompilerParams(vmem_limit_bytes=8 << 20),
    )(*held(*remote, space=pltpu.HBM), *held(*args))


def groups_of(level, steps, count):
    groups, seen = [], set()
    for i in range(count):
        if i in seen:
            continue
        members = [i]
        for step in steps:
            members += [m ^ step for m in members]
        members.sort(key=lambda m: (m >> level) & (len(members) - 1))
        seen.update(members)
        groups.append(members)
    return groups


def gather(block, level, step, count):
    return lax.all_gather(block, "leaf", axis_index_groups=groups_of(level, (step,), count))


def exchange(group, level, steps, count):
    return lax.all_to_all(group, "leaf", 0, 0, axis_index_groups=groups_of(level, steps, count))


def local(particles, counts, neighbours, pattern, kernels):
    vmem, hbm, dma = pltpu.VMEM, pltpu.HBM, pltpu.SemaphoreType.DMA
    group_out = hbm((4, CELLS, COEFFS), F32)
    block_out = vmem((CELLS, COEFFS), F32)
    pair_out = vmem((2, CELLS, COEFFS), F32)
    half_out = vmem((4, SLOTS, LANES), F32)
    moments = vmem((ORDER,) * 3 + (LEAVES,), F32)
    count = lax.axis_size("leaf")
    inputs = (particles, counts, neighbours.transpose(1, 0, 2), pattern[0], *tile_maps(1), *tile_maps(2))
    block, wx, wy, wz, dense, *landed = call(
        p2m_kernel,
        (
            block_out,
            vmem((ORDER, SLOTS, LEAVES), F32),
            vmem((ORDER, SLOTS, LEAVES), F32),
            vmem((SLOTS, ORDER, LEAVES), F32),
            vmem((4, SLOTS, LEAVES), F32),
            *[vmem(x.shape, x.dtype) for x in inputs],
        ),
        (),
        (
            vmem((2 * ORDER * SLOTS, LANES), F32),
            vmem((SLOTS, ORDER, ORDER, LEAVES), F32),
            moments,
            dma((len(inputs),)),
        ),
        (10_000_000, 2_000_000),
        inputs,
    )
    counts, neighbours, pattern = landed[1:4]
    mid_maps, inner_maps = landed[4:6], landed[6:8]
    merging = (block_out, dma((4,)))
    width = lax.axis_size("near")
    forward = [(i, i + 1) for i in range(width - 1)]
    group, first = call(
        merge_first_kernel,
        (block_out, block_out),
        (gather(block, 0, 1, count),),
        (),
        (1_000_000, 1_000_000),
    )
    group, second, last_half = call(
        merge_second_kernel,
        (group_out, block_out, half_out),
        (gather(group, 1, 2, count), *mid_maps, dense),
        merging,
        (1_000_000, 1_000_000),
    )
    got = exchange(group, 2, (7, 8), count)
    before = lax.ppermute(last_half, "near", forward)
    group, mid_sources, first_half = call(
        merge_mid_kernel,
        (group_out, pair_out, half_out),
        (got, *inner_maps, dense, before),
        merging,
        (1_000_000, 1_000_000),
    )
    got = exchange(group, 4, (16, 56), count)
    after = lax.ppermute(first_half, "near", [(t, s) for s, t in forward])
    (near,) = call(
        near_kernel,
        (vmem((SLOTS, LEAVES), F32),),
        (first_half, last_half, before, after, neighbours),
        (vmem((NEAR_LEAVES, 4, SLOTS, LANES), F32),),
        (2_000_000_000, 8_000_000),
    )
    select, gathered, fetched = call(
        select_kernel,
        (
            vmem((256, 256), BF16),
            vmem((256, COEFFS), F32),
            vmem((AHEAD,) + kernels.shape[1:], BF16),
        ),
        (pattern, block, first, second, mid_sources),
        (
            vmem((CELLS, 256), jnp.int32),
            vmem((5 * CELLS, COEFFS), F32),
            dma((AHEAD,)),
        ),
        (1_000_000_000, 8_000_000),
        (kernels,),
    )
    potential, local_exp = call(
        final_kernel,
        (hbm((SLOTS, 1, LEAVES), F32), hbm((CELLS, COEFFS), F32)),
        (got, *mid_maps, select, gathered, fetched, wx, wy, wz, near, counts),
        (
            vmem((2 * CELLS, COEFFS), F32),
            moments,
            vmem((OPERATORS - AHEAD,) + kernels.shape[1:], BF16),
            block_out,
            vmem((SLOTS, 1, LEAVES), F32),
            dma((OPERATORS + 1,)),
        ),
        (1_000_000_000, 8_000_000),
        (kernels,),
    )
    return potential, local_exp[None]


def solution(mesh):
    placed = (
        P(None, None, "leaf", "near"),
        P("leaf", "near"),
        P("leaf", None, "near"),
        P("leaf", None, None, "near"),
        P(),
    )
    return jax.shard_map(
        local,
        mesh=mesh,
        in_specs=placed,
        out_specs=(P(None, "leaf", "near"), P("leaf", "near", None)),
        check_vma=False,
    )
```

time: 61.5 us -> 55.1 us (0.90)
  the two profiles are of different devices: /device:TPU:4 before, /device:TPU:6 now
where the time goes in v1:
time: 55.1 us; the launch traced here: 54.7 us
  starting transfers between devices  21.1 us (38%)
  blocking collectives  12.5 us (23%)
  Pallas kernels  10.8 us (20%)
  waiting for transfers between devices  9.66 us (18%)
  between operations  0.69 us (1%)
    all_to_all x2, starting transfers between devices, exchange(): lax.all_to_all(group, 'leaf', 0, 0, axis_index_groups=groups_of(level, st...  17.3 us
    all_gather x2, blocking collectives, gather(): lax.all_gather(block, 'leaf', axis_index_groups=groups_of(level, (step,),...  12.5 us
    pallas_call x7, Pallas kernels, call(): pl.pallas_call(kernel, out_shape=outs, in_specs=[apart] * len(remote) + [...  10.8 us
    all_to_all x2, waiting for transfers between devices, exchange(): lax.all_to_all(group, 'leaf', 0, 0, axis_index_groups=groups_of(level, st...  6.03 us
    ppermute x1, waiting for transfers between devices, local(): before = lax.ppermute(last_half, 'near', forward)  3.31 us
    ppermute x1, starting transfers between devices, local(): before = lax.ppermute(last_half, 'near', forward)  1.91 us
    ppermute x1, starting transfers between devices, local(): after = lax.ppermute(first_half, 'near', [(t, s) for s, t in forward])  1.91 us
  transfers between devices with their start and end apart: 4, of which 4 were waited for; matrix products, arithmetic and copies ran while one was open for 0% of the time, Pallas kernels for 4%

profile of v1, /device:TPU:6, one launch (start us, length us, event | category | flops | bytes accessed | tf_op | source)
XLA Modules:
  0.0 54.7 jit_solution(62066544022517611)
XLA Ops:
  0.6 2.6 %shard_map.104 = (f32[32,512]{1,0:T(8,128)S(1)}, f32[8,16,256]{2,1,0:T(8,128)S(1)}, f32[8,16,256]{2,1,0:T(8,128)S(1)}, f32[16,8,256]{2,1,0:T(8,128)S(1)}, f32[4,...) custom-call(f32[4,16,1,256]{3,2,1,0:T(1,128)} %refs_0_.1, ...), custom_call_target="tpu_custom_call" | custom-call | flops 10000000 | bytes 2000000 | tf_op jit(solution)/shard_map/pallas_call | solution.py:391
  3.3 5.3 %all-gather = f32[64,512]{1,0:T(8,128)S(1)} all-gather(f32[32,512]{1,0:T(8,128)S(1)} %get-tuple-element.27.block), channel_id=2, replica_groups={{0,8},{16,24},{32,40},{48,56},{64,72},{80,88},{96,104},{112,120},{128,1..., dimensions={0}, use_global_device_ids=true | all-gather | bytes 196608 | tf_op jit(solution)/shard_map/all_gather | solution.py:417
  8.6 0.1 shard_map.105
  8.7 7.3 %all-gather.1 = f32[64,512]{1,0:T(8,128)S(1)} all-gather(f32[32,512]{1,0:T(8,128)S(1)} %get-tuple-element.28), channel_id=3, replica_groups={{0,16},{8,24},{32,48},{40,56},{64,80},{72,88},{96,112},{104,120},{128,1..., dimensions={0}, use_global_device_ids=true | all-gather | bytes 196608 | tf_op jit(solution)/shard_map/all_gather | solution.py:417
  15.9 0.9 %shard_map.106 = (f32[4,32,512]{2,1,0:T(8,128)}, f32[32,512]{1,0:T(8,128)S(1)}, f32[4,16,128]{2,1,0:T(8,128)S(1)}) custom-call(f32[2,32,512]{2,1,0:T(8,128)S(1)} %bitcast.5, bf16[256,128]{1,0:T(8,128)(2,1)S(1)} %get-tuple-element.29.high, bf16[256,128]{1,0:T(8,128)(2,1)S(1)} %get-tuple-element.30.low, f32[4,16,256]{2,1,0:T(8,128)S(1)} %get-tuple-element.31.dense), custom_call_target="tpu_custom_call" | custom-call | flops 1000000 | bytes 1000000 | tf_op jit(solution)/shard_map/pallas_call | solution.py:391
  16.9 10.3 %all-to-all-start = ((f32[4,32,512]{2,1,0:T(8,128)}), f32[4,32,512]{2,1,0:T(8,128)S(1)}, u32[]{:S(2)}, u32[]{:S(2)}) async-start(f32[4,32,512]{2,1,0:T(8,128)} %get-tuple-element.32), calls=%async_computation | async-start | bytes 524288 | tf_op jit(solution)/shard_map/all_to_all | solution.py:421
  27.2 1.9 %collective-permute-start = (f32[4,16,128]{2,1,0:T(8,128)S(1)}, f32[4,16,128]{2,1,0:T(8,128)S(1)}, u32[]{:S(2)}, u32[]{:S(2)}) collective-permute-start(f32[4,16,128]{2,1,0:T(8,128)S(1)} %get-tuple-element.35.mine_last), channel_id=1, source_target_pairs={{0,1},{1,2},{2,3},{3,4},{4,5},{5,6},{6,7},{8,9},{9,10},{10,11},{11... | collective-permute-start | bytes 98312 | tf_op jit(solution)/shard_map/ppermute | solution.py:473
  29.1 3.3 %collective-permute-done.before = f32[4,16,128]{2,1,0:T(8,128)S(1)} collective-permute-done((f32[4,16,128]{2,1,0:T(8,128)S(1)}, f32[4,16,128]{2,1,0:T(8,128)S(1)}, u32[]{:S(2)}, u32[]{:S(2)}) %collective-permute-start) | collective-permute-done | bytes 32800 | tf_op jit(solution)/shard_map/ppermute | solution.py:473
  32.4 1.8 %all-to-all-done.got = f32[4,32,512]{2,1,0:T(8,128)S(1)} async-done(((f32[4,32,512]{2,1,0:T(8,128)}), f32[4,32,512]{2,1,0:T(8,128)S(1)}, u32[]{:S(2)}, u32[]{:S(2)}) %all-to-all-start) | async-done | bytes 262176 | tf_op jit(solution)/shard_map/all_to_all | solution.py:421
  34.2 1.1 %shard_map.107 = (f32[4,32,512]{2,1,0:T(8,128)}, f32[2,32,512]{2,1,0:T(8,128)S(1)}, f32[4,16,128]{2,1,0:T(8,128)S(1)}) custom-call(f32[4,32,512]{2,1,0:T(8,128)S(1)} %all-to-all-done.got, bf16[256,128]{1,0:T(8,128)(2,1)S(1)} %get-tuple-element.33.high, bf16[256,128]{1,0:T(8,128)(2,1)S(1)} %get-tuple-element.34.low, ...), custom_call_target="tpu_custom_call" | custom-call | flops 1000000 | bytes 1000000 | tf_op jit(solution)/shard_map/pallas_call | solution.py:391
  35.3 7.0 %all-to-all-start.1 = ((f32[4,32,512]{2,1,0:T(8,128)}), f32[4,32,512]{2,1,0:T(8,128)S(1)}, u32[]{:S(2)}, u32[]{:S(2)}) async-start(f32[4,32,512]{2,1,0:T(8,128)} %get-tuple-element.36), calls=%async_computation.1 | async-start | bytes 524288 | tf_op jit(solution)/shard_map/all_to_all | solution.py:421
  42.2 1.9 %collective-permute-start.1 = (f32[4,16,128]{2,1,0:T(8,128)S(1)}, f32[4,16,128]{2,1,0:T(8,128)S(1)}, u32[]{:S(2)}, u32[]{:S(2)}) collective-permute-start(f32[4,16,128]{2,1,0:T(8,128)S(1)} %get-tuple-element.47.mine_first), channel_id=1, source_target_pairs={{1,0},{2,1},{3,2},{4,3},{5,4},{6,5},{7,6},{9,8},{10,9},{11,10},{12... | collective-permute-start | bytes 98312 | tf_op jit(solution)/shard_map/ppermute | solution.py:482
  44.2 1.2 %shard_map.108 = (bf16[256,256]{1,0:T(8,128)(2,1)S(1)}, f32[256,512]{1,0:T(8,128)S(1)}, bf16[2,512,512]{2,1,0:T(8,128)(2,1)S(1)}) custom-call(bf16[8,512,512]{2,1,0:T(8,128)(2,1)} %kernels.3, s32[7,32,32]{2,1,0:T(8,128)S(1)} %get-tuple-element.37.pattern, f32[32,512]{1,0:T(8,128)S(1)} %get-tuple-element.27.block, f32[32,512]{1,0:T(8,128)S(1)} %get-tuple-element.38.first, ...), custom_call_target="tpu_custom_call" | custom-call | flops 1000000000 | bytes 8000000 | tf_op jit(solution)/shard_map/pallas_call | solution.py:391
  45.4 0.3 collective-permute-done.1.after
  45.7 1.1 %shard_map.109.near = f32[16,256]{1,0:T(8,128)S(1)} custom-call(f32[4,16,128]{2,1,0:T(8,128)S(1)} %get-tuple-element.47.mine_first, f32[4,16,128]{2,1,0:T(8,128)S(1)} %get-tuple-element.35.mine_last, f32[4,16,128]{2,1,0:T(8,128)S(1)} %collective-permute-done.before, f32[4,16,128]{2,1,0:T(8,128)S(1)} %collective-permute-done.1.after, ...), custom_call_target="tpu_custom_call" | custom-call | flops 2000000000 | bytes 8000000 | tf_op jit(solution)/shard_map/pallas_call | solution.py:391
  46.8 4.2 %all-to-all-done.1.got = f32[4,32,512]{2,1,0:T(8,128)S(1)} async-done(((f32[4,32,512]{2,1,0:T(8,128)}), f32[4,32,512]{2,1,0:T(8,128)S(1)}, u32[]{:S(2)}, u32[]{:S(2)}) %all-to-all-start.1) | async-done | bytes 262176 | tf_op jit(solution)/shard_map/all_to_all | solution.py:421
  51.1 3.6 %shard_map.110 = (f32[16,1,256]{2,1,0:T(1,128)}, f32[32,512]{1,0:T(8,128)}) custom-call(bf16[8,512,512]{2,1,0:T(8,128)(2,1)} %kernels.3, f32[4,32,512]{2,1,0:T(8,128)S(1)} %all-to-all-done.1.got, bf16[256,128]{1,0:T(8,128)(2,1)S(1)} %get-tuple-element.29.high, bf16[256,128]{1,0:T(8,128)(2,1)S(1)} %get-tuple-element.30.low, ...), custom_call_target="tpu_custom_call" | custom-call | flops 1000000000 | bytes 8000000 | tf_op jit(solution)/shard_map/pallas_call | solution.py:391
Async XLA Ops:
  16.9 17.3 %all-to-all-start = ((f32[4,32,512]{2,1,0:T(8,128)}), f32[4,32,512]{2,1,0:T(8,128)S(1)}, u32[]{:S(2)}, u32[]{:S(2)}) async-start(f32[4,32,512]{2,1,0:T(8,128)} %get-tuple-element.32), calls=%async_computation | async-start | bytes 524288 | tf_op jit(solution)/shard_map/all_to_all | solution.py:421
  27.2 5.2 %collective-permute-start = (f32[4,16,128]{2,1,0:T(8,128)S(1)}, f32[4,16,128]{2,1,0:T(8,128)S(1)}, u32[]{:S(2)}, u32[]{:S(2)}) collective-permute-start(f32[4,16,128]{2,1,0:T(8,128)S(1)} %get-tuple-element.35.mine_last), channel_id=1, source_target_pairs={{0,1},{1,2},{2,3},{3,4},{4,5},{5,6},{6,7},{8,9},{9,10},{10,11},{11... | collective-permute-start | bytes 98312 | tf_op jit(solution)/shard_map/ppermute | solution.py:473
  35.3 15.8 %all-to-all-start.1 = ((f32[4,32,512]{2,1,0:T(8,128)}), f32[4,32,512]{2,1,0:T(8,128)S(1)}, u32[]{:S(2)}, u32[]{:S(2)}) async-start(f32[4,32,512]{2,1,0:T(8,128)} %get-tuple-element.36), calls=%async_computation.1 | async-start | bytes 524288 | tf_op jit(solution)/shard_map/all_to_all | solution.py:421
  42.2 3.5 %collective-permute-start.1 = (f32[4,16,128]{2,1,0:T(8,128)S(1)}, f32[4,16,128]{2,1,0:T(8,128)S(1)}, u32[]{:S(2)}, u32[]{:S(2)}) collective-permute-start(f32[4,16,128]{2,1,0:T(8,128)S(1)} %get-tuple-element.47.mine_first), channel_id=1, source_target_pairs={{1,0},{2,1},{3,2},{4,3},{5,4},{6,5},{7,6},{9,8},{10,9},{11,10},{12... | collective-permute-start | bytes 98312 | tf_op jit(solution)/shard_map/ppermute | solution.py:482

commit v2 on v1

--- a/solution.py
+++ b/solution.py
@@ -234,7 +234,7 @@
         copy.wait()
 
 
-def merge_mid_kernel(got, high, low, dense, before, group, sources, first_half, block, done):
+def merge_mid_kernel(got, high, low, dense, before, gathered, group, sources, first_half, block, done):
     mine = own_place(2)
     pairs = map_inner(
         [(tiles_of(got, 2 * t), tiles_of(got, 2 * t + 1)) for t in range(2)], high[...], low[...]
@@ -247,7 +247,12 @@
         copy.wait()
 
 
-def near_kernel(mine_first, mine_last, before, after, lists, near, sources):
+def near_kernel(kernels, mine_first, mine_last, before, after, lists, near, fetched, sources, done):
+    copies = [
+        pltpu.make_async_copy(kernels.at[o], fetched.at[o], done.at[o]) for o in range(AHEAD)
+    ]
+    for copy in copies:
+        copy.start()
     lane = iota((8, LANES), 1)
     for g in range(2):
         here = slice(g * LANES, (g + 1) * LANES)
@@ -282,30 +287,28 @@
             return total
 
         near[:, here] = lax.fori_loop(0, NEAR_LEAVES, pair, jnp.zeros((SLOTS, LANES), F32))
-
-
-def select_kernel(kernels, pattern, block, first, second, mid_sources, select, gathered, fetched, codes, stack, done):
-    copies = [
-        pltpu.make_async_copy(kernels.at[o], fetched.at[o], done.at[o]) for o in range(AHEAD)
-    ]
-    for copy in copies:
-        copy.start()
+    for copy in copies:
+        copy.wait()
+
+
+def select_kernel(pattern, block, first, second, select, gathered, codes, stack):
     codes[...] = jnp.zeros(codes.shape, jnp.int32)
     for v in range(LEVELS + 1):
         codes[:, v * CELLS : (v + 1) * CELLS] = pattern[v]
     for o in range(OPERATORS):
         rows = slice(o * CELLS, (o + 1) * CELLS)
         select[rows, :] = (codes[...] == o + 1).astype(F32).astype(BF16)
-    stack[0:CELLS] = block[...]
-    stack[CELLS : 2 * CELLS] = first[...]
-    stack[2 * CELLS : 3 * CELLS] = second[...]
-    for i in range(2):
-        stack[(3 + i) * CELLS : (4 + i) * CELLS] = mid_sources[i]
+    for v, source in enumerate((block, first, second)):
+        stack[v * CELLS : (v + 1) * CELLS] = source[...]
     high, low = split(stack[...])
-    known = select[:, : 5 * CELLS]
+    known = select[:, : 3 * CELLS]
     gathered[...] = mm(known, high) + mm(known, low)
-    for copy in copies:
-        copy.wait()
+
+
+def add_kernel(select, before, mid_sources, gathered):
+    high, low = split(mid_sources[...].reshape(2 * CELLS, COEFFS))
+    known = select[:, 3 * CELLS : 5 * CELLS]
+    gathered[...] = before[...] + (mm(known, high) + mm(known, low))
 
 
 def final_kernel(
@@ -471,36 +474,34 @@
     )
     got = exchange(group, 2, (7, 8), count)
     before = lax.ppermute(last_half, "near", forward)
+    select, gathered = call(
+        select_kernel,
+        (vmem((256, 256), BF16), vmem((256, COEFFS), F32)),
+        (pattern, block, first, second),
+        (vmem((CELLS, 256), jnp.int32), vmem((3 * CELLS, COEFFS), F32)),
+        (1_000_000_000, 4_000_000),
+    )
     group, mid_sources, first_half = call(
         merge_mid_kernel,
         (group_out, pair_out, half_out),
-        (got, *inner_maps, dense, before),
+        (got, *inner_maps, dense, before, gathered),
         merging,
         (1_000_000, 1_000_000),
     )
-    got = exchange(group, 4, (16, 56), count)
+    got = exchange(group, 4, (24, 48), count)
     after = lax.ppermute(first_half, "near", [(t, s) for s, t in forward])
-    (near,) = call(
+    (gathered,) = call(
+        add_kernel,
+        (vmem((256, COEFFS), F32),),
+        (select, gathered, mid_sources),
+        cost=(500_000_000, 2_000_000),
+    )
+    near, fetched = call(
         near_kernel,
-        (vmem((SLOTS, LEAVES), F32),),
+        (vmem((SLOTS, LEAVES), F32), vmem((AHEAD,) + kernels.shape[1:], BF16)),
         (first_half, last_half, before, after, neighbours),
-        (vmem((NEAR_LEAVES, 4, SLOTS, LANES), F32),),
+        (vmem((NEAR_LEAVES, 4, SLOTS, LANES), F32), dma((AHEAD,))),
         (2_000_000_000, 8_000_000),
-    )
-    select, gathered, fetched = call(
-        select_kernel,
-        (
-            vmem((256, 256), BF16),
-            vmem((256, COEFFS), F32),
-            vmem((AHEAD,) + kernels.shape[1:], BF16),
-        ),
-        (pattern, block, first, second, mid_sources),
-        (
-            vmem((CELLS, 256), jnp.int32),
-            vmem((5 * CELLS, COEFFS), F32),
-            dma((AHEAD,)),
-        ),
-        (1_000_000_000, 8_000_000),
         (kernels,),
     )
     potential, local_exp = call(

time: 55.1 us -> 54.5 us (0.989)
    ppermute x1, waiting for transfers between devices: 0.33 us -> 1.24 us  [local(): after = lax.ppermute(first_half, 'near', [(t, s) for s, t in forward])]
    all_to_all x2, waiting for transfers between devices: 6.03 us -> 5.29 us  [exchange(): lax.all_to_all(group, 'leaf', 0, 0, axis_index_groups=groups_of(level, st...]
    pallas_call x7 -> x8, Pallas kernels: 10.8 us -> 10.3 us  [call(): pl.pallas_call(kernel, out_shape=outs, in_specs=[apart] * len(remote) + [...]
where the time goes in v2:
time: 54.5 us; the launch traced here: 54.1 us
  starting transfers between devices  21.1 us (39%)
  blocking collectives  12.5 us (23%)
  Pallas kernels  10.3 us (19%)
  waiting for transfers between devices  9.47 us (17%)
  between operations  0.7 us (1%)
    all_to_all x2, starting transfers between devices, exchange(): lax.all_to_all(group, 'leaf', 0, 0, axis_index_groups=groups_of(level, st...  17.3 us
    all_gather x2, blocking collectives, gather(): lax.all_gather(block, 'leaf', axis_index_groups=groups_of(level, (step,),...  12.5 us
    pallas_call x8, Pallas kernels, call(): pl.pallas_call(kernel, out_shape=outs, in_specs=[apart] * len(remote) + [...  10.3 us
    all_to_all x2, waiting for transfers between devices, exchange(): lax.all_to_all(group, 'leaf', 0, 0, axis_index_groups=groups_of(level, st...  5.29 us
    ppermute x1, waiting for transfers between devices, local(): before = lax.ppermute(last_half, 'near', forward)  2.94 us
    ppermute x1, starting transfers between devices, local(): before = lax.ppermute(last_half, 'near', forward)  1.91 us
    ppermute x1, starting transfers between devices, local(): after = lax.ppermute(first_half, 'near', [(t, s) for s, t in forward])  1.91 us
    ppermute x1, waiting for transfers between devices, local(): after = lax.ppermute(first_half, 'near', [(t, s) for s, t in forward])  1.24 us
  transfers between devices with their start and end apart: 4, of which 4 were waited for; matrix products, arithmetic and copies ran while one was open for 0% of the time, Pallas kernels for 4%

profile of v2, /device:TPU:6, one launch (start us, length us, event | category | flops | bytes accessed | tf_op | source)
XLA Modules:
  0.0 54.1 jit_solution(5869818486135232568)
XLA Ops:
  0.6 2.7 %shard_map.104 = (f32[32,512]{1,0:T(8,128)S(1)}, f32[8,16,256]{2,1,0:T(8,128)S(1)}, f32[8,16,256]{2,1,0:T(8,128)S(1)}, f32[16,8,256]{2,1,0:T(8,128)S(1)}, f32[4,...) custom-call(f32[4,16,1,256]{3,2,1,0:T(1,128)} %refs_0_.1, ...), custom_call_target="tpu_custom_call" | custom-call | flops 10000000 | bytes 2000000 | tf_op jit(solution)/shard_map/pallas_call | solution.py:394
  3.3 5.3 %all-gather = f32[64,512]{1,0:T(8,128)S(1)} all-gather(f32[32,512]{1,0:T(8,128)S(1)} %get-tuple-element.28.block), channel_id=2, replica_groups={{0,8},{16,24},{32,40},{48,56},{64,72},{80,88},{96,104},{112,120},{128,1..., dimensions={0}, use_global_device_ids=true | all-gather | bytes 196608 | tf_op jit(solution)/shard_map/all_gather | solution.py:420
  8.6 0.1 shard_map.105
  8.7 7.3 %all-gather.1 = f32[64,512]{1,0:T(8,128)S(1)} all-gather(f32[32,512]{1,0:T(8,128)S(1)} %get-tuple-element.29), channel_id=3, replica_groups={{0,16},{8,24},{32,48},{40,56},{64,80},{72,88},{96,112},{104,120},{128,1..., dimensions={0}, use_global_device_ids=true | all-gather | bytes 196608 | tf_op jit(solution)/shard_map/all_gather | solution.py:420
  15.9 0.9 %shard_map.106 = (f32[4,32,512]{2,1,0:T(8,128)}, f32[32,512]{1,0:T(8,128)S(1)}, f32[4,16,128]{2,1,0:T(8,128)S(1)}) custom-call(f32[2,32,512]{2,1,0:T(8,128)S(1)} %bitcast.5, bf16[256,128]{1,0:T(8,128)(2,1)S(1)} %get-tuple-element.30.high, bf16[256,128]{1,0:T(8,128)(2,1)S(1)} %get-tuple-element.31.low, f32[4,16,256]{2,1,0:T(8,128)S(1)} %get-tuple-element.32.dense), custom_call_target="tpu_custom_call" | custom-call | flops 1000000 | bytes 1000000 | tf_op jit(solution)/shard_map/pallas_call | solution.py:394
  16.9 10.3 %all-to-all-start = ((f32[4,32,512]{2,1,0:T(8,128)}), f32[4,32,512]{2,1,0:T(8,128)S(1)}, u32[]{:S(2)}, u32[]{:S(2)}) async-start(f32[4,32,512]{2,1,0:T(8,128)} %get-tuple-element.33), calls=%async_computation | async-start | bytes 524288 | tf_op jit(solution)/shard_map/all_to_all | solution.py:424
  27.2 1.9 %collective-permute-start = (f32[4,16,128]{2,1,0:T(8,128)S(1)}, f32[4,16,128]{2,1,0:T(8,128)S(1)}, u32[]{:S(2)}, u32[]{:S(2)}) collective-permute-start(f32[4,16,128]{2,1,0:T(8,128)S(1)} %get-tuple-element.36.mine_last), channel_id=1, source_target_pairs={{0,1},{1,2},{2,3},{3,4},{4,5},{5,6},{6,7},{8,9},{9,10},{10,11},{11... | collective-permute-start | bytes 98312 | tf_op jit(solution)/shard_map/ppermute | solution.py:476
  29.1 0.4 shard_map.107
  29.4 2.9 %collective-permute-done.before = f32[4,16,128]{2,1,0:T(8,128)S(1)} collective-permute-done((f32[4,16,128]{2,1,0:T(8,128)S(1)}, f32[4,16,128]{2,1,0:T(8,128)S(1)}, u32[]{:S(2)}, u32[]{:S(2)}) %collective-permute-start) | collective-permute-done | bytes 32800 | tf_op jit(solution)/shard_map/ppermute | solution.py:476
  32.4 1.8 %all-to-all-done.got = f32[4,32,512]{2,1,0:T(8,128)S(1)} async-done(((f32[4,32,512]{2,1,0:T(8,128)}), f32[4,32,512]{2,1,0:T(8,128)S(1)}, u32[]{:S(2)}, u32[]{:S(2)}) %all-to-all-start) | async-done | bytes 262176 | tf_op jit(solution)/shard_map/all_to_all | solution.py:424
  34.2 1.1 %shard_map.108 = (f32[4,32,512]{2,1,0:T(8,128)}, f32[2,32,512]{2,1,0:T(8,128)S(1)}, f32[4,16,128]{2,1,0:T(8,128)S(1)}) custom-call(f32[4,32,512]{2,1,0:T(8,128)S(1)} %all-to-all-done.got, bf16[256,128]{1,0:T(8,128)(2,1)S(1)} %get-tuple-element.34.high, bf16[256,128]{1,0:T(8,128)(2,1)S(1)} %get-tuple-element.35.low, ...), custom_call_target="tpu_custom_call" | custom-call | flops 1000000 | bytes 1000000 | tf_op jit(solution)/shard_map/pallas_call | solution.py:394
  35.3 7.0 %all-to-all-start.1 = ((f32[4,32,512]{2,1,0:T(8,128)}), f32[4,32,512]{2,1,0:T(8,128)S(1)}, u32[]{:S(2)}, u32[]{:S(2)}) async-start(f32[4,32,512]{2,1,0:T(8,128)} %get-tuple-element.41), calls=%async_computation.1 | async-start | bytes 524288 | tf_op jit(solution)/shard_map/all_to_all | solution.py:424
  42.2 1.9 %collective-permute-start.1 = (f32[4,16,128]{2,1,0:T(8,128)S(1)}, f32[4,16,128]{2,1,0:T(8,128)S(1)}, u32[]{:S(2)}, u32[]{:S(2)}) collective-permute-start(f32[4,16,128]{2,1,0:T(8,128)S(1)} %get-tuple-element.44.mine_first), channel_id=1, source_target_pairs={{1,0},{2,1},{3,2},{4,3},{5,4},{6,5},{7,6},{9,8},{10,9},{11,10},{12... | collective-permute-start | bytes 98312 | tf_op jit(solution)/shard_map/ppermute | solution.py:492
  44.2 0.3 shard_map.109.gathered
  44.5 1.2 %collective-permute-done.1.after = f32[4,16,128]{2,1,0:T(8,128)S(1)} collective-permute-done((f32[4,16,128]{2,1,0:T(8,128)S(1)}, f32[4,16,128]{2,1,0:T(8,128)S(1)}, u32[]{:S(2)}, u32[]{:S(2)}) %collective-permute-start.1) | collective-permute-done | bytes 32800 | tf_op jit(solution)/shard_map/ppermute | solution.py:492
  45.7 1.2 %shard_map.110 = (f32[16,256]{1,0:T(8,128)S(1)}, bf16[2,512,512]{2,1,0:T(8,128)(2,1)S(1)}) custom-call(bf16[8,512,512]{2,1,0:T(8,128)(2,1)} %kernels.3, f32[4,16,128]{2,1,0:T(8,128)S(1)} %get-tuple-element.44.mine_first, f32[4,16,128]{2,1,0:T(8,128)S(1)} %get-tuple-element.36.mine_last, f32[4,16,128]{2,1,0:T(8,128)S(1)} %collective-permute-done.before, ...), custom_call_target="tpu_custom_call" | custom-call | flops 2000000000 | bytes 8000000 | tf_op jit(solution)/shard_map/pallas_call | solution.py:394
  47.0 3.5 %all-to-all-done.1.got = f32[4,32,512]{2,1,0:T(8,128)S(1)} async-done(((f32[4,32,512]{2,1,0:T(8,128)}), f32[4,32,512]{2,1,0:T(8,128)S(1)}, u32[]{:S(2)}, u32[]{:S(2)}) %all-to-all-start.1) | async-done | bytes 262176 | tf_op jit(solution)/shard_map/all_to_all | solution.py:424
  50.5 3.6 %shard_map.111 = (f32[16,1,256]{2,1,0:T(1,128)}, f32[32,512]{1,0:T(8,128)}) custom-call(bf16[8,512,512]{2,1,0:T(8,128)(2,1)} %kernels.3, f32[4,32,512]{2,1,0:T(8,128)S(1)} %all-to-all-done.1.got, bf16[256,128]{1,0:T(8,128)(2,1)S(1)} %get-tuple-element.30.high, bf16[256,128]{1,0:T(8,128)(2,1)S(1)} %get-tuple-element.31.low, ...), custom_call_target="tpu_custom_call" | custom-call | flops 1000000000 | bytes 8000000 | tf_op jit(solution)/shard_map/pallas_call | solution.py:394
Async XLA Ops:
  16.9 17.3 %all-to-all-start = ((f32[4,32,512]{2,1,0:T(8,128)}), f32[4,32,512]{2,1,0:T(8,128)S(1)}, u32[]{:S(2)}, u32[]{:S(2)}) async-start(f32[4,32,512]{2,1,0:T(8,128)} %get-tuple-element.33), calls=%async_computation | async-start | bytes 524288 | tf_op jit(solution)/shard_map/all_to_all | solution.py:424
  27.2 5.2 %collective-permute-start = (f32[4,16,128]{2,1,0:T(8,128)S(1)}, f32[4,16,128]{2,1,0:T(8,128)S(1)}, u32[]{:S(2)}, u32[]{:S(2)}) collective-permute-start(f32[4,16,128]{2,1,0:T(8,128)S(1)} %get-tuple-element.36.mine_last), channel_id=1, source_target_pairs={{0,1},{1,2},{2,3},{3,4},{4,5},{5,6},{6,7},{8,9},{9,10},{10,11},{11... | collective-permute-start | bytes 98312 | tf_op jit(solution)/shard_map/ppermute | solution.py:476
  35.3 15.2 %all-to-all-start.1 = ((f32[4,32,512]{2,1,0:T(8,128)}), f32[4,32,512]{2,1,0:T(8,128)S(1)}, u32[]{:S(2)}, u32[]{:S(2)}) async-start(f32[4,32,512]{2,1,0:T(8,128)} %get-tuple-element.41), calls=%async_computation.1 | async-start | bytes 524288 | tf_op jit(solution)/shard_map/all_to_all | solution.py:424
  42.2 3.5 %collective-permute-start.1 = (f32[4,16,128]{2,1,0:T(8,128)S(1)}, f32[4,16,128]{2,1,0:T(8,128)S(1)}, u32[]{:S(2)}, u32[]{:S(2)}) collective-permute-start(f32[4,16,128]{2,1,0:T(8,128)S(1)} %get-tuple-element.44.mine_first), channel_id=1, source_target_pairs={{1,0},{2,1},{3,2},{4,3},{5,4},{6,5},{7,6},{9,8},{10,9},{11,10},{12... | collective-permute-start | bytes 98312 | tf_op jit(solution)/shard_map/ppermute | solution.py:492

commit v3 on v2

--- a/solution.py
+++ b/solution.py
@@ -468,11 +468,11 @@
     group, second, last_half = call(
         merge_second_kernel,
         (group_out, block_out, half_out),
-        (gather(group, 1, 2, count), *mid_maps, dense),
+        (gather(group, 1, 3, count), *mid_maps, dense),
         merging,
         (1_000_000, 1_000_000),
     )
-    got = exchange(group, 2, (7, 8), count)
+    got = exchange(group, 2, (6, 8), count)
     before = lax.ppermute(last_half, "near", forward)
     select, gathered = call(
         select_kernel,

time: 54.5 us -> 53.9 us (0.989); the launches traced: 54.1 us -> 52.9 us
  starting transfers between devices: 21.1 us -> 17.4 us
  blocking collectives: 12.5 us -> 13.8 us
  waiting for transfers between devices: 9.47 us -> 10.6 us
    all_to_all x2, starting transfers between devices: 17.3 us -> 13.6 us  [exchange(): lax.all_to_all(group, 'leaf', 0, 0, axis_index_groups=groups_of(level, st...]
    all_gather x2, blocking collectives: 12.5 us -> 13.8 us  [gather(): lax.all_gather(block, 'leaf', axis_index_groups=groups_of(level, (step,),...]
    all_to_all x2, waiting for transfers between devices: 5.29 us -> 6.43 us  [exchange(): lax.all_to_all(group, 'leaf', 0, 0, axis_index_groups=groups_of(level, st...]
where the time goes in v3:
time: 53.9 us; the launch traced here: 52.9 us
  starting transfers between devices  17.4 us (32%)
  blocking collectives  13.8 us (26%)
  waiting for transfers between devices  10.6 us (20%)
  Pallas kernels  10.3 us (19%)
  between operations  0.7 us (1%)
    all_gather x2, blocking collectives, gather(): lax.all_gather(block, 'leaf', axis_index_groups=groups_of(level, (step,),...  13.8 us
    all_to_all x2, starting transfers between devices, exchange(): lax.all_to_all(group, 'leaf', 0, 0, axis_index_groups=groups_of(level, st...  13.6 us
    pallas_call x8, Pallas kernels, call(): pl.pallas_call(kernel, out_shape=outs, in_specs=[apart] * len(remote) + [...  10.3 us
    all_to_all x2, waiting for transfers between devices, exchange(): lax.all_to_all(group, 'leaf', 0, 0, axis_index_groups=groups_of(level, st...  6.43 us
    ppermute x1, waiting for transfers between devices, local(): before = lax.ppermute(last_half, 'near', forward)  2.94 us
    ppermute x1, starting transfers between devices, local(): before = lax.ppermute(last_half, 'near', forward)  1.91 us
    ppermute x1, starting transfers between devices, local(): after = lax.ppermute(first_half, 'near', [(t, s) for s, t in forward])  1.91 us
    ppermute x1, waiting for transfers between devices, local(): after = lax.ppermute(first_half, 'near', [(t, s) for s, t in forward])  1.24 us
  transfers between devices with their start and end apart: 4, of which 4 were waited for; matrix products, arithmetic and copies ran while one was open for 0% of the time, Pallas kernels for 4%

profile of v3, /device:TPU:6, one launch (start us, length us, event | category | flops | bytes accessed | tf_op | source)
XLA Modules:
  0.0 52.9 jit_solution(3222402079344259523)
XLA Ops:
  0.6 2.7 %shard_map.104 = (f32[32,512]{1,0:T(8,128)S(1)}, f32[8,16,256]{2,1,0:T(8,128)S(1)}, f32[8,16,256]{2,1,0:T(8,128)S(1)}, f32[16,8,256]{2,1,0:T(8,128)S(1)}, f32[4,...) custom-call(f32[4,16,1,256]{3,2,1,0:T(1,128)} %refs_0_.1, ...), custom_call_target="tpu_custom_call" | custom-call | flops 10000000 | bytes 2000000 | tf_op jit(solution)/shard_map/pallas_call | solution.py:394
  3.3 5.3 %all-gather = f32[64,512]{1,0:T(8,128)S(1)} all-gather(f32[32,512]{1,0:T(8,128)S(1)} %get-tuple-element.28.block), channel_id=2, replica_groups={{0,8},{16,24},{32,40},{48,56},{64,72},{80,88},{96,104},{112,120},{128,1..., dimensions={0}, use_global_device_ids=true | all-gather | bytes 196608 | tf_op jit(solution)/shard_map/all_gather | solution.py:420
  8.6 0.1 shard_map.105
  8.7 8.6 %all-gather.1 = f32[64,512]{1,0:T(8,128)S(1)} all-gather(f32[32,512]{1,0:T(8,128)S(1)} %get-tuple-element.29), channel_id=3, replica_groups={{0,24},{8,16},{32,56},{40,48},{64,88},{72,80},{96,120},{104,112},{128,1..., dimensions={0}, use_global_device_ids=true | all-gather | bytes 196608 | tf_op jit(solution)/shard_map/all_gather | solution.py:420
  17.2 0.9 %shard_map.106 = (f32[4,32,512]{2,1,0:T(8,128)}, f32[32,512]{1,0:T(8,128)S(1)}, f32[4,16,128]{2,1,0:T(8,128)S(1)}) custom-call(f32[2,32,512]{2,1,0:T(8,128)S(1)} %bitcast.5, bf16[256,128]{1,0:T(8,128)(2,1)S(1)} %get-tuple-element.30.high, bf16[256,128]{1,0:T(8,128)(2,1)S(1)} %get-tuple-element.31.low, f32[4,16,256]{2,1,0:T(8,128)S(1)} %get-tuple-element.32.dense), custom_call_target="tpu_custom_call" | custom-call | flops 1000000 | bytes 1000000 | tf_op jit(solution)/shard_map/pallas_call | solution.py:394
  18.2 7.6 %all-to-all-start = ((f32[4,32,512]{2,1,0:T(8,128)}), f32[4,32,512]{2,1,0:T(8,128)S(1)}, u32[]{:S(2)}, u32[]{:S(2)}) async-start(f32[4,32,512]{2,1,0:T(8,128)} %get-tuple-element.33), calls=%async_computation | async-start | bytes 524288 | tf_op jit(solution)/shard_map/all_to_all | solution.py:424
  25.8 1.9 %collective-permute-start = (f32[4,16,128]{2,1,0:T(8,128)S(1)}, f32[4,16,128]{2,1,0:T(8,128)S(1)}, u32[]{:S(2)}, u32[]{:S(2)}) collective-permute-start(f32[4,16,128]{2,1,0:T(8,128)S(1)} %get-tuple-element.36.mine_last), channel_id=1, source_target_pairs={{0,1},{1,2},{2,3},{3,4},{4,5},{5,6},{6,7},{8,9},{9,10},{10,11},{11... | collective-permute-start | bytes 98312 | tf_op jit(solution)/shard_map/ppermute | solution.py:476
  27.7 0.4 shard_map.107
  28.1 2.9 %collective-permute-done.before = f32[4,16,128]{2,1,0:T(8,128)S(1)} collective-permute-done((f32[4,16,128]{2,1,0:T(8,128)S(1)}, f32[4,16,128]{2,1,0:T(8,128)S(1)}, u32[]{:S(2)}, u32[]{:S(2)}) %collective-permute-start) | collective-permute-done | bytes 32800 | tf_op jit(solution)/shard_map/ppermute | solution.py:476
  31.0 2.3 %all-to-all-done.got = f32[4,32,512]{2,1,0:T(8,128)S(1)} async-done(((f32[4,32,512]{2,1,0:T(8,128)}), f32[4,32,512]{2,1,0:T(8,128)S(1)}, u32[]{:S(2)}, u32[]{:S(2)}) %all-to-all-start) | async-done | bytes 262176 | tf_op jit(solution)/shard_map/all_to_all | solution.py:424
  33.3 1.1 %shard_map.108 = (f32[4,32,512]{2,1,0:T(8,128)}, f32[2,32,512]{2,1,0:T(8,128)S(1)}, f32[4,16,128]{2,1,0:T(8,128)S(1)}) custom-call(f32[4,32,512]{2,1,0:T(8,128)S(1)} %all-to-all-done.got, bf16[256,128]{1,0:T(8,128)(2,1)S(1)} %get-tuple-element.34.high, bf16[256,128]{1,0:T(8,128)(2,1)S(1)} %get-tuple-element.35.low, ...), custom_call_target="tpu_custom_call" | custom-call | flops 1000000 | bytes 1000000 | tf_op jit(solution)/shard_map/pallas_call | solution.py:394
  34.4 6.0 %all-to-all-start.1 = ((f32[4,32,512]{2,1,0:T(8,128)}), f32[4,32,512]{2,1,0:T(8,128)S(1)}, u32[]{:S(2)}, u32[]{:S(2)}) async-start(f32[4,32,512]{2,1,0:T(8,128)} %get-tuple-element.41), calls=%async_computation.1 | async-start | bytes 524288 | tf_op jit(solution)/shard_map/all_to_all | solution.py:424
  40.4 1.9 %collective-permute-start.1 = (f32[4,16,128]{2,1,0:T(8,128)S(1)}, f32[4,16,128]{2,1,0:T(8,128)S(1)}, u32[]{:S(2)}, u32[]{:S(2)}) collective-permute-start(f32[4,16,128]{2,1,0:T(8,128)S(1)} %get-tuple-element.44.mine_first), channel_id=1, source_target_pairs={{1,0},{2,1},{3,2},{4,3},{5,4},{6,5},{7,6},{9,8},{10,9},{11,10},{12... | collective-permute-start | bytes 98312 | tf_op jit(solution)/shard_map/ppermute | solution.py:492
  42.3 0.3 shard_map.109.gathered
  42.6 1.2 %collective-permute-done.1.after = f32[4,16,128]{2,1,0:T(8,128)S(1)} collective-permute-done((f32[4,16,128]{2,1,0:T(8,128)S(1)}, f32[4,16,128]{2,1,0:T(8,128)S(1)}, u32[]{:S(2)}, u32[]{:S(2)}) %collective-permute-start.1) | collective-permute-done | bytes 32800 | tf_op jit(solution)/shard_map/ppermute | solution.py:492
  43.8 1.2 %shard_map.110 = (f32[16,256]{1,0:T(8,128)S(1)}, bf16[2,512,512]{2,1,0:T(8,128)(2,1)S(1)}) custom-call(bf16[8,512,512]{2,1,0:T(8,128)(2,1)} %kernels.3, f32[4,16,128]{2,1,0:T(8,128)S(1)} %get-tuple-element.44.mine_first, f32[4,16,128]{2,1,0:T(8,128)S(1)} %get-tuple-element.36.mine_last, f32[4,16,128]{2,1,0:T(8,128)S(1)} %collective-permute-done.before, ...), custom_call_target="tpu_custom_call" | custom-call | flops 2000000000 | bytes 8000000 | tf_op jit(solution)/shard_map/pallas_call | solution.py:394
  45.1 4.2 %all-to-all-done.1.got = f32[4,32,512]{2,1,0:T(8,128)S(1)} async-done(((f32[4,32,512]{2,1,0:T(8,128)}), f32[4,32,512]{2,1,0:T(8,128)S(1)}, u32[]{:S(2)}, u32[]{:S(2)}) %all-to-all-start.1) | async-done | bytes 262176 | tf_op jit(solution)/shard_map/all_to_all | solution.py:424
  49.2 3.6 %shard_map.111 = (f32[16,1,256]{2,1,0:T(1,128)}, f32[32,512]{1,0:T(8,128)}) custom-call(bf16[8,512,512]{2,1,0:T(8,128)(2,1)} %kernels.3, f32[4,32,512]{2,1,0:T(8,128)S(1)} %all-to-all-done.1.got, bf16[256,128]{1,0:T(8,128)(2,1)S(1)} %get-tuple-element.30.high, bf16[256,128]{1,0:T(8,128)(2,1)S(1)} %get-tuple-element.31.low, ...), custom_call_target="tpu_custom_call" | custom-call | flops 1000000000 | bytes 8000000 | tf_op jit(solution)/shard_map/pallas_call | solution.py:394
Async XLA Ops:
  18.2 15.1 %all-to-all-start = ((f32[4,32,512]{2,1,0:T(8,128)}), f32[4,32,512]{2,1,0:T(8,128)S(1)}, u32[]{:S(2)}, u32[]{:S(2)}) async-start(f32[4,32,512]{2,1,0:T(8,128)} %get-tuple-element.33), calls=%async_computation | async-start | bytes 524288 | tf_op jit(solution)/shard_map/all_to_all | solution.py:424
  25.8 5.2 %collective-permute-start = (f32[4,16,128]{2,1,0:T(8,128)S(1)}, f32[4,16,128]{2,1,0:T(8,128)S(1)}, u32[]{:S(2)}, u32[]{:S(2)}) collective-permute-start(f32[4,16,128]{2,1,0:T(8,128)S(1)} %get-tuple-element.36.mine_last), channel_id=1, source_target_pairs={{0,1},{1,2},{2,3},{3,4},{4,5},{5,6},{6,7},{8,9},{9,10},{10,11},{11... | collective-permute-start | bytes 98312 | tf_op jit(solution)/shard_map/ppermute | solution.py:476
  34.4 14.9 %all-to-all-start.1 = ((f32[4,32,512]{2,1,0:T(8,128)}), f32[4,32,512]{2,1,0:T(8,128)S(1)}, u32[]{:S(2)}, u32[]{:S(2)}) async-start(f32[4,32,512]{2,1,0:T(8,128)} %get-tuple-element.41), calls=%async_computation.1 | async-start | bytes 524288 | tf_op jit(solution)/shard_map/all_to_all | solution.py:424
  40.4 3.5 %collective-permute-start.1 = (f32[4,16,128]{2,1,0:T(8,128)S(1)}, f32[4,16,128]{2,1,0:T(8,128)S(1)}, u32[]{:S(2)}, u32[]{:S(2)}) collective-permute-start(f32[4,16,128]{2,1,0:T(8,128)S(1)} %get-tuple-element.44.mine_first), channel_id=1, source_target_pairs={{1,0},{2,1},{3,2},{4,3},{5,4},{6,5},{7,6},{9,8},{10,9},{11,10},{12... | collective-permute-start | bytes 98312 | tf_op jit(solution)/shard_map/ppermute | solution.py:492

commit v4 on v3

--- a/solution.py
+++ b/solution.py
@@ -19,7 +19,7 @@
 RIM = 8
 LANES = 128
 HALF = 64
-AHEAD = 2
+AHEAD = 3
 
 F32, BF16 = jnp.float32, jnp.bfloat16
 

time: 53.9 us -> 54 us (level)
  the two profiles are of different devices: /device:TPU:6 before, /device:TPU:70 now
where the time goes in v4:
time: 54 us; the launch traced here: 53.6 us
  starting transfers between devices  21.1 us (39%)
  blocking collectives  10.8 us (20%)
  Pallas kernels  10.5 us (19%)
  waiting for transfers between devices  10.4 us (19%)
  between operations  0.7 us (1%)
    all_to_all x2, starting transfers between devices, exchange(): lax.all_to_all(group, 'leaf', 0, 0, axis_index_groups=groups_of(level, st...  17.3 us
    all_gather x2, blocking collectives, gather(): lax.all_gather(block, 'leaf', axis_index_groups=groups_of(level, (step,),...  10.8 us
    pallas_call x8, Pallas kernels, call(): pl.pallas_call(kernel, out_shape=outs, in_specs=[apart] * len(remote) + [...  10.5 us
    all_to_all x2, waiting for transfers between devices, exchange(): lax.all_to_all(group, 'leaf', 0, 0, axis_index_groups=groups_of(level, st...  6.26 us
    ppermute x1, waiting for transfers between devices, local(): before = lax.ppermute(last_half, 'near', forward)  2.94 us
    ppermute x1, starting transfers between devices, local(): before = lax.ppermute(last_half, 'near', forward)  1.91 us
    ppermute x1, starting transfers between devices, local(): after = lax.ppermute(first_half, 'near', [(t, s) for s, t in forward])  1.91 us
    ppermute x1, waiting for transfers between devices, local(): after = lax.ppermute(first_half, 'near', [(t, s) for s, t in forward])  1.24 us
  transfers between devices with their start and end apart: 4, of which 4 were waited for; matrix products, arithmetic and copies ran while one was open for 0% of the time, Pallas kernels for 4%

profile of v4, /device:TPU:70, one launch (start us, length us, event | category | flops | bytes accessed | tf_op | source)
XLA Modules:
  0.0 53.6 jit_solution(4263173317004519731)
XLA Ops:
  0.6 2.7 %shard_map.104 = (f32[32,512]{1,0:T(8,128)S(1)}, f32[8,16,256]{2,1,0:T(8,128)S(1)}, f32[8,16,256]{2,1,0:T(8,128)S(1)}, f32[16,8,256]{2,1,0:T(8,128)S(1)}, f32[4,...) custom-call(f32[4,16,1,256]{3,2,1,0:T(1,128)} %refs_0_.1, ...), custom_call_target="tpu_custom_call" | custom-call | flops 10000000 | bytes 2000000 | tf_op jit(solution)/shard_map/pallas_call | solution.py:394
  3.3 4.9 %all-gather = f32[64,512]{1,0:T(8,128)S(1)} all-gather(f32[32,512]{1,0:T(8,128)S(1)} %get-tuple-element.28.block), channel_id=2, replica_groups={{0,8},{16,24},{32,40},{48,56},{64,72},{80,88},{96,104},{112,120},{128,1..., dimensions={0}, use_global_device_ids=true | all-gather | bytes 196608 | tf_op jit(solution)/shard_map/all_gather | solution.py:420
  8.2 0.1 shard_map.105
  8.4 5.9 %all-gather.1 = f32[64,512]{1,0:T(8,128)S(1)} all-gather(f32[32,512]{1,0:T(8,128)S(1)} %get-tuple-element.29), channel_id=3, replica_groups={{0,24},{8,16},{32,56},{40,48},{64,88},{72,80},{96,120},{104,112},{128,1..., dimensions={0}, use_global_device_ids=true | all-gather | bytes 196608 | tf_op jit(solution)/shard_map/all_gather | solution.py:420
  14.3 0.9 %shard_map.106 = (f32[4,32,512]{2,1,0:T(8,128)}, f32[32,512]{1,0:T(8,128)S(1)}, f32[4,16,128]{2,1,0:T(8,128)S(1)}) custom-call(f32[2,32,512]{2,1,0:T(8,128)S(1)} %bitcast.5, bf16[256,128]{1,0:T(8,128)(2,1)S(1)} %get-tuple-element.30.high, bf16[256,128]{1,0:T(8,128)(2,1)S(1)} %get-tuple-element.31.low, f32[4,16,256]{2,1,0:T(8,128)S(1)} %get-tuple-element.32.dense), custom_call_target="tpu_custom_call" | custom-call | flops 1000000 | bytes 1000000 | tf_op jit(solution)/shard_map/pallas_call | solution.py:394
  15.2 11.3 %all-to-all-start = ((f32[4,32,512]{2,1,0:T(8,128)}), f32[4,32,512]{2,1,0:T(8,128)S(1)}, u32[]{:S(2)}, u32[]{:S(2)}) async-start(f32[4,32,512]{2,1,0:T(8,128)} %get-tuple-element.33), calls=%async_computation | async-start | bytes 524288 | tf_op jit(solution)/shard_map/all_to_all | solution.py:424
  26.5 1.9 %collective-permute-start = (f32[4,16,128]{2,1,0:T(8,128)S(1)}, f32[4,16,128]{2,1,0:T(8,128)S(1)}, u32[]{:S(2)}, u32[]{:S(2)}) collective-permute-start(f32[4,16,128]{2,1,0:T(8,128)S(1)} %get-tuple-element.36.mine_last), channel_id=1, source_target_pairs={{0,1},{1,2},{2,3},{3,4},{4,5},{5,6},{6,7},{8,9},{9,10},{10,11},{11... | collective-permute-start | bytes 98312 | tf_op jit(solution)/shard_map/ppermute | solution.py:476
  28.4 0.4 shard_map.107
  28.7 2.9 %collective-permute-done.before = f32[4,16,128]{2,1,0:T(8,128)S(1)} collective-permute-done((f32[4,16,128]{2,1,0:T(8,128)S(1)}, f32[4,16,128]{2,1,0:T(8,128)S(1)}, u32[]{:S(2)}, u32[]{:S(2)}) %collective-permute-start) | collective-permute-done | bytes 32800 | tf_op jit(solution)/shard_map/ppermute | solution.py:476
  31.7 2.3 %all-to-all-done.got = f32[4,32,512]{2,1,0:T(8,128)S(1)} async-done(((f32[4,32,512]{2,1,0:T(8,128)}), f32[4,32,512]{2,1,0:T(8,128)S(1)}, u32[]{:S(2)}, u32[]{:S(2)}) %all-to-all-start) | async-done | bytes 262176 | tf_op jit(solution)/shard_map/all_to_all | solution.py:424
  34.0 1.1 %shard_map.108 = (f32[4,32,512]{2,1,0:T(8,128)}, f32[2,32,512]{2,1,0:T(8,128)S(1)}, f32[4,16,128]{2,1,0:T(8,128)S(1)}) custom-call(f32[4,32,512]{2,1,0:T(8,128)S(1)} %all-to-all-done.got, bf16[256,128]{1,0:T(8,128)(2,1)S(1)} %get-tuple-element.34.high, bf16[256,128]{1,0:T(8,128)(2,1)S(1)} %get-tuple-element.35.low, ...), custom_call_target="tpu_custom_call" | custom-call | flops 1000000 | bytes 1000000 | tf_op jit(solution)/shard_map/pallas_call | solution.py:394
  35.0 6.0 %all-to-all-start.1 = ((f32[4,32,512]{2,1,0:T(8,128)}), f32[4,32,512]{2,1,0:T(8,128)S(1)}, u32[]{:S(2)}, u32[]{:S(2)}) async-start(f32[4,32,512]{2,1,0:T(8,128)} %get-tuple-element.41), calls=%async_computation.1 | async-start | bytes 524288 | tf_op jit(solution)/shard_map/all_to_all | solution.py:424
  41.0 1.9 %collective-permute-start.1 = (f32[4,16,128]{2,1,0:T(8,128)S(1)}, f32[4,16,128]{2,1,0:T(8,128)S(1)}, u32[]{:S(2)}, u32[]{:S(2)}) collective-permute-start(f32[4,16,128]{2,1,0:T(8,128)S(1)} %get-tuple-element.44.mine_first), channel_id=1, source_target_pairs={{1,0},{2,1},{3,2},{4,3},{5,4},{6,5},{7,6},{9,8},{10,9},{11,10},{12... | collective-permute-start | bytes 98312 | tf_op jit(solution)/shard_map/ppermute | solution.py:492
  43.0 0.3 shard_map.109.gathered
  43.3 1.2 %collective-permute-done.1.after = f32[4,16,128]{2,1,0:T(8,128)S(1)} collective-permute-done((f32[4,16,128]{2,1,0:T(8,128)S(1)}, f32[4,16,128]{2,1,0:T(8,128)S(1)}, u32[]{:S(2)}, u32[]{:S(2)}) %collective-permute-start.1) | collective-permute-done | bytes 32800 | tf_op jit(solution)/shard_map/ppermute | solution.py:492
  44.5 1.4 %shard_map.110 = (f32[16,256]{1,0:T(8,128)S(1)}, bf16[3,512,512]{2,1,0:T(8,128)(2,1)S(1)}) custom-call(bf16[8,512,512]{2,1,0:T(8,128)(2,1)} %kernels.3, f32[4,16,128]{2,1,0:T(8,128)S(1)} %get-tuple-element.44.mine_first, f32[4,16,128]{2,1,0:T(8,128)S(1)} %get-tuple-element.36.mine_last, f32[4,16,128]{2,1,0:T(8,128)S(1)} %collective-permute-done.before, ...), custom_call_target="tpu_custom_call" | custom-call | flops 2000000000 | bytes 8000000 | tf_op jit(solution)/shard_map/pallas_call | solution.py:394
  45.9 4.0 %all-to-all-done.1.got = f32[4,32,512]{2,1,0:T(8,128)S(1)} async-done(((f32[4,32,512]{2,1,0:T(8,128)}), f32[4,32,512]{2,1,0:T(8,128)S(1)}, u32[]{:S(2)}, u32[]{:S(2)}) %all-to-all-start.1) | async-done | bytes 262176 | tf_op jit(solution)/shard_map/all_to_all | solution.py:424
  49.9 3.7 %shard_map.111 = (f32[16,1,256]{2,1,0:T(1,128)}, f32[32,512]{1,0:T(8,128)}) custom-call(bf16[8,512,512]{2,1,0:T(8,128)(2,1)} %kernels.3, f32[4,32,512]{2,1,0:T(8,128)S(1)} %all-to-all-done.1.got, bf16[256,128]{1,0:T(8,128)(2,1)S(1)} %get-tuple-element.30.high, bf16[256,128]{1,0:T(8,128)(2,1)S(1)} %get-tuple-element.31.low, ...), custom_call_target="tpu_custom_call" | custom-call | flops 1000000000 | bytes 8000000 | tf_op jit(solution)/shard_map/pallas_call | solution.py:394
Async XLA Ops:
  15.2 18.8 %all-to-all-start = ((f32[4,32,512]{2,1,0:T(8,128)}), f32[4,32,512]{2,1,0:T(8,128)S(1)}, u32[]{:S(2)}, u32[]{:S(2)}) async-start(f32[4,32,512]{2,1,0:T(8,128)} %get-tuple-element.33), calls=%async_computation | async-start | bytes 524288 | tf_op jit(solution)/shard_map/all_to_all | solution.py:424
  26.5 5.2 %collective-permute-start = (f32[4,16,128]{2,1,0:T(8,128)S(1)}, f32[4,16,128]{2,1,0:T(8,128)S(1)}, u32[]{:S(2)}, u32[]{:S(2)}) collective-permute-start(f32[4,16,128]{2,1,0:T(8,128)S(1)} %get-tuple-element.36.mine_last), channel_id=1, source_target_pairs={{0,1},{1,2},{2,3},{3,4},{4,5},{5,6},{6,7},{8,9},{9,10},{10,11},{11... | collective-permute-start | bytes 98312 | tf_op jit(solution)/shard_map/ppermute | solution.py:476
  35.0 14.9 %all-to-all-start.1 = ((f32[4,32,512]{2,1,0:T(8,128)}), f32[4,32,512]{2,1,0:T(8,128)S(1)}, u32[]{:S(2)}, u32[]{:S(2)}) async-start(f32[4,32,512]{2,1,0:T(8,128)} %get-tuple-element.41), calls=%async_computation.1 | async-start | bytes 524288 | tf_op jit(solution)/shard_map/all_to_all | solution.py:424
  41.0 3.5 %collective-permute-start.1 = (f32[4,16,128]{2,1,0:T(8,128)S(1)}, f32[4,16,128]{2,1,0:T(8,128)S(1)}, u32[]{:S(2)}, u32[]{:S(2)}) collective-permute-start(f32[4,16,128]{2,1,0:T(8,128)S(1)} %get-tuple-element.44.mine_first), channel_id=1, source_target_pairs={{1,0},{2,1},{3,2},{4,3},{5,4},{6,5},{7,6},{9,8},{10,9},{11,10},{12... | collective-permute-start | bytes 98312 | tf_op jit(solution)/shard_map/ppermute | solution.py:492
